TPU v7x, 256 devices: a whole 4x4x8 slice. The times are simulated.
256 devices in a mesh: ep: 32 (over z, y_lo, core), fsdp: 8 (over y_hi, x).
Axes of the slice: x: 4, y: 4 (y_hi: 2, y_lo: 2; y = y_hi * 2 + y_lo), z: 8, core: 2. Of those that a mesh axis runs over, the one named last changes fastest.
Arguments:
- tokens: bfloat16 [4096, 7168], P('ep', 'fsdp'), may hold values from -6 to 6
- cotangent: bfloat16 [4096, 7168], P('ep', 'fsdp'), may hold values from -6 to 6
- route_gates: float32 [4096, 2], P('ep'), may hold values from 0.2 to 1
- expert_ids: int32 [4096, 2], P('ep'), may hold values from 0 to 7, all different within a row; in each aligned block of 128 rows (0 to 127, 128 to 255, ...) at most 64 rows name the same one
- w_gate: bfloat16 [7168, 8192], P('fsdp', 'ep'), may hold values from -0.0625 to 0.0625
- w_up: bfloat16 [7168, 8192], P('fsdp', 'ep'), may hold values from -0.0625 to 0.0625
- w_down: bfloat16 [7168, 8192], P('fsdp', 'ep'), may hold values from -0.1875 to 0.1875
Outputs:
- grad_tokens: bfloat16 [4096, 7168], P('ep', 'fsdp')
- grad_gate: bfloat16 [7168, 8192], P('fsdp', 'ep')
- grad_up: bfloat16 [7168, 8192], P('fsdp', 'ep')
- grad_down: bfloat16 [7168, 8192], P('fsdp', 'ep')
Inputs may be any that keep to these rules, and one draw needn't show every extreme that they name: `expert_ids`: each token names 2 different experts; among the 128 tokens of one block no expert is named more than 64 times, a bound that some block reaches.
All inputs are finite; a program needn't handle non-finite values.
Results may differ from a plain program's by a relative error of at most 0.0064.
Values may be sent and summed in bfloat16 or wider, within the bound.
A program may use at most 64 MiB of HBM per device.

v0:
```python
import jax
import jax.numpy as jnp
from jax import lax
from jax.sharding import PartitionSpec as P

EXPERTS = 8
CAP = 64


def cross_dot(left, right):
    return lax.dot_general(
        left, right, (((0,), (0,)), ((), ())), preferred_element_type=jnp.float32
    )


def right_dot(left, right):
    return lax.dot_general(
        left, right, (((1,), (1,)), ((), ())), preferred_element_type=jnp.float32
    )


def activations(pre_gate, pre_up, grad_hidden):
    sigmoid_gate = jax.nn.sigmoid(pre_gate)
    activated = pre_gate * sigmoid_gate
    hidden = (activated * pre_up).astype(jnp.bfloat16)
    grad_a = (grad_hidden * pre_up * sigmoid_gate * (1.0 + pre_gate * (1.0 - sigmoid_gate))).astype(
        jnp.bfloat16
    )
    grad_u = (grad_hidden * activated).astype(jnp.bfloat16)
    return (hidden, grad_a, grad_u)


def body(tokens, cotangent, route_gates, expert_ids, w_gate, w_up, w_down):
    tok_count, width = tokens.shape
    top_count = expert_ids.shape[1]
    ep_count = lax.axis_size("ep")
    split_ways = ep_count // EXPERTS
    pair_count = tok_count * top_count
    slot_total = EXPERTS * CAP
    row_count = ep_count * CAP
    flat_ids = expert_ids.reshape(pair_count)
    onehot = (flat_ids[:, None] == jnp.arange(EXPERTS, dtype=jnp.int32)[None, :]).astype(jnp.int32)
    slot_index = jnp.sum(jnp.cumsum(onehot, axis=0) * onehot, axis=1) - 1
    destination = flat_ids * CAP + slot_index
    placed = (destination[:, None] == jnp.arange(slot_total, dtype=jnp.int32)[None, :]).astype(
        jnp.float32
    )
    owner_token = jnp.arange(pair_count, dtype=jnp.int32) // top_count
    token_of = (owner_token[:, None] == jnp.arange(tok_count, dtype=jnp.int32)[None, :]).astype(
        jnp.float32
    )
    selector = jnp.dot(
        placed.T, token_of, precision=lax.Precision.HIGHEST, preferred_element_type=jnp.float32
    ).astype(jnp.bfloat16)
    slot_gate = jnp.dot(
        placed.T,
        route_gates.reshape(pair_count),
        precision=lax.Precision.HIGHEST,
        preferred_element_type=jnp.float32,
    )
    send_x = jnp.dot(selector, tokens, preferred_element_type=jnp.float32).astype(jnp.bfloat16)
    picked_c = jnp.dot(selector, cotangent, preferred_element_type=jnp.float32)
    send_c = (slot_gate[:, None] * picked_c).astype(jnp.bfloat16)
    stacked = jnp.stack((send_x, send_c)).reshape(2, EXPERTS, CAP, width)
    outgoing = jnp.broadcast_to(stacked[:, :, None], (2, EXPERTS, split_ways, CAP, width))
    arrived = lax.all_to_all(
        outgoing.reshape(2, ep_count, CAP, width), "ep", split_axis=1, concat_axis=1, tiled=True
    )
    rows_x = arrived[0].reshape(row_count, width)
    rows_c = arrived[1].reshape(row_count, width)
    pre_gate, pre_up, grad_hidden = lax.psum(
        (
            jnp.dot(rows_x, w_gate, preferred_element_type=jnp.float32),
            jnp.dot(rows_x, w_up, preferred_element_type=jnp.float32),
            jnp.dot(rows_c, w_down, preferred_element_type=jnp.float32),
        ),
        "fsdp",
    )
    hidden, grad_a, grad_u = activations(pre_gate, pre_up, grad_hidden)
    row_term = (right_dot(grad_a, w_gate) + right_dot(grad_u, w_up)).astype(jnp.bfloat16)
    grad_gate = cross_dot(rows_x, grad_a).astype(jnp.bfloat16)
    grad_up = cross_dot(rows_x, grad_u).astype(jnp.bfloat16)
    grad_down = cross_dot(rows_c, hidden).astype(jnp.bfloat16)
    returned = lax.all_to_all(
        row_term.reshape(ep_count, CAP, width), "ep", split_axis=0, concat_axis=0, tiled=True
    )
    slot_sums = jnp.sum(
        returned.reshape(EXPERTS, split_ways, CAP, width).astype(jnp.float32), axis=1
    )
    slot_rows = slot_sums.reshape(slot_total, width)
    route_rows = slot_rows[destination].reshape(tok_count, top_count, width)
    grad_tokens = jnp.sum(route_rows, axis=1).astype(jnp.bfloat16)
    return (grad_tokens, grad_gate, grad_up, grad_down)


def solution(mesh):
    placed = (
        P("ep", "fsdp"),
        P("ep", "fsdp"),
        P("ep", None),
        P("ep", None),
        P("fsdp", "ep"),
        P("fsdp", "ep"),
        P("fsdp", "ep"),
    )
    return jax.shard_map(
        body,
        mesh=mesh,
        in_specs=placed,
        out_specs=(P("ep", "fsdp"), P("fsdp", "ep"), P("fsdp", "ep"), P("fsdp", "ep")),
        check_vma=False,
    )
```

profile of v0, /device:TPU:1, one launch (start us, length us, event | category | flops | bytes accessed | tf_op | source)
XLA Modules:
  0.0 462.0 jit_solution(4994211981276225759)
XLA Ops:
  7.2 0.9 copy.15
  8.3 0.1 reshape.102
  8.4 0.6 reduce-window.6
  9.0 0.2 slice_reduce_fusion
  9.4 0.8 copy.17
  10.3 0.4 convolution_convert_fusion.4
  10.7 0.3 fusion.1
  11.1 1.3 convolution_convert_fusion
  12.4 0.4 multiply_convert_fusion.3
  12.8 0.2 maximum_bitcast_fusion
  13.0 0.2 copy.18
  13.2 1.1 broadcast_in_dim.5
  14.3 173.9 %all_to_all.10 = bf16[2,32,64,896]{3,2,0,1:T(8,128)(2,1)S(1)} all-to-all(bf16[2,32,64,896]{3,2,0,1:T(8,128)(2,1)S(1)} %bitcast.46), channel_id=1, replica_groups=mesh['ep'=32,'fsdp'=8] {'ep'}, dimensions={1} | all-to-all | bytes 14680064 | tf_op jit(solution)/shard_map/all_to_all | solution.py:66
  188.2 1.2 fusion.9
  189.4 3.1 fusion.11
  192.6 2.6 fusion.12
  195.1 2.6 fusion.10
  197.7 149.4 %all-reduce.3.cloned.1.call-done = (f32[2048,256]{1,0:T(8,128)}, f32[2048,256]{1,0:T(8,128)}, f32[2048,256]{1,0:T(8,128)}) async-done(((f32[2048,256]{1,0:T(8,128)}, f32[2048,256]{1,0:T(8,128)}, f32[2048,256]{1,0:T(8,128)}), (f32[2048,256]{1,0:T(8,128)}, f32[2048,256]{1,0:T(8,128)}, f32[2048,256]{1,0:T(8,128)})) %all-reduce.3.cloned.1.call-update) | async-done | bytes 6291472 | tf_op jit(solution)/shard_map/psum | solution.py:71
  347.2 3.8 multiply_convert_fusion.1
  351.0 1.3 fusion.13
  352.3 3.2 add_convert_fusion
  355.5 8.1 %all-to-all-start.1 = ((bf16[32,64,896]{2,1,0:T(8,128)(2,1)}), bf16[32,64,896]{2,1,0:T(8,128)(2,1)}, u32[]{:S(2)}, u32[]{:S(2)}) async-start(bf16[32,64,896]{2,1,0:T(8,128)(2,1)} %bitcast.49), calls=%async_computation.1 | async-start | bytes 7340032 | tf_op jit(solution)/shard_map/all_to_all | solution.py:84
  363.8 4.1 convolution_convert_fusion.2
  368.0 1.9 convolution_convert_fusion.3
  370.0 0.8 copy-done.5
  370.8 0.6 copy-done.6
  371.4 2.1 convolution_convert_fusion.1
  373.5 75.4 %all-to-all-done.1 = bf16[32,64,896]{2,1,0:T(8,128)(2,1)} async-done(((bf16[32,64,896]{2,1,0:T(8,128)(2,1)}), bf16[32,64,896]{2,1,0:T(8,128)(2,1)}, u32[]{:S(2)}, u32[]{:S(2)}) %all-to-all-start.1) | async-done | bytes 3670048 | tf_op jit(solution)/shard_map/all_to_all | solution.py:84
  448.9 2.7 convert_reduce_fusion
  451.7 1.1 gather_fusion
  452.8 0.5 reshape.108
  453.3 1.9 reduce_sum.29
  (34 shorter events, 0.9 us)
Async XLA Ops:
  7.2 185.4 %copy-start = (bf16[896,256]{1,0:T(8,128)(2,1)S(1)}, bf16[896,256]{1,0:T(8,128)(2,1)}, u32[]{:S(2)}) copy-start(bf16[896,256]{1,0:T(8,128)(2,1)} %param.11) | copy-start | bytes 1376260
  7.2 5.2 %copy-start.9 = (bf16[128,896]{1,0:T(8,128)(2,1)S(1)}, bf16[128,896]{1,0:T(8,128)(2,1)}, u32[]{:S(2)}) copy-start(bf16[128,896]{1,0:T(8,128)(2,1)} %param.8) | copy-start | bytes 688132
  7.2 340.0 %all-reduce.3.cloned.1.call-start = ((), (), s32[]{:S(2)}) async-start(), calls=%async_computation.2 | async-start | bytes 12582912 | tf_op jit(solution)/shard_map/psum | solution.py:71
  188.2 1.2 copy-start.7
  189.4 3.2 copy-start.1
  189.4 5.8 %copy-start.3 = (bf16[1,32,64,896]{3,2,0,1:T(8,128)(2,1)}, bf16[1,32,64,896]{3,2,0,1:T(8,128)(2,1)S(1)}, u32[]{:S(2)}) copy-start(bf16[1,32,64,896]{3,2,0,1:T(8,128)(2,1)S(1)} %get-tuple-element.7) | copy-start | bytes 11010052
  192.6 2.6 copy-start.8
  355.5 8.1 %copy-start.10 = (s32[128,2]{0,1:T(2,128)S(1)}, s32[128,2]{0,1:T(2,128)}, u32[]{:S(2)}) copy-start(s32[128,2]{0,1:T(2,128)} %param.10) | copy-start | bytes 3076
  355.5 93.4 %all-to-all-start.1 = ((bf16[32,64,896]{2,1,0:T(8,128)(2,1)}), bf16[32,64,896]{2,1,0:T(8,128)(2,1)}, u32[]{:S(2)}, u32[]{:S(2)}) async-start(bf16[32,64,896]{2,1,0:T(8,128)(2,1)} %bitcast.49), calls=%async_computation.1 | async-start | bytes 7340032 | tf_op jit(solution)/shard_map/all_to_all | solution.py:84
  363.8 4.1 copy-start.2
  368.0 2.0 copy-start.4
  368.0 2.9 copy-start.5
  368.0 3.5 copy-start.6
Sparse Core Ops, SparseCore 0:
  197.9 149.2 all-reduce.2
where the time goes:
time: 462 us
  waiting for transfers between devices  225 us (49%)
  blocking collectives  174 us (38%)
  matrix products  23.4 us (5%)
  between operations  14.2 us (3%)
  other arithmetic  9.36 us (2%)
  local copies, waits for them, and re-layouts  8.21 us (2%)
  starting transfers between devices  8.1 us (2%)
    all_to_all x1, blocking collectives, body(): lax.all_to_all(outgoing.reshape(2, ep_count, CAP, width), 'ep', split_axi...  174 us
    psum x1, waiting for transfers between devices, body(): lax.psum((jnp.dot(rows_x, w_gate, preferred_element_type=jnp.float32), jn...  149 us
    all_to_all x1, waiting for transfers between devices, body(): lax.all_to_all(row_term.reshape(ep_count, CAP, width), 'ep', split_axis=0...  75.4 us
  transfers between devices with their start and end apart: 2, of which 2 were waited for; matrix products, arithmetic and copies ran while one was open for 2% of the time, Pallas kernels for 0%

commit v1 on v0

v1 whole, which is shorter than its diff:
```python
import jax
import jax.numpy as jnp
from jax import lax
from jax.experimental import pallas as pl
from jax.experimental.pallas import tpu as pltpu
from jax.sharding import PartitionSpec as P

EXPERTS = 8
CAP = 64
TOK = 128
FEAT = 896
HID = 256
MESH = pl.DeviceIdType.MESH

SHIFT = (0, -1, 1, -2, 2, -3, 3, 4)
CHUNKS = ((0, 1), (1, 2), (3, 2), (5, 2), (7, 1))
SEMS = 224

ARRIVAL = (0.0, 10.0, 20.0, 30.0, 36.0)
STEPS = (
    ("zx", -3.0, 0.0),
    ("zc", 0.0, 0.0),
    ("yx", 1.5, 2.5),
    ("yc", 1.6, 5.0),
    ("mx", 2.5, 5.0),
    ("mc", 3.0, 5.5),
    ("sum_far", 5.0, 6.5),
    ("sum_near", 6.5, 8.5),
    ("act", 8.5, 9.5),
    ("spread", 10.5, 10.5),
    ("relay", 12.5, 12.5),
    ("rows", 14.5, 13.5),
    ("pair", 16.5, 14.0),
    ("back", 18.5, 16.5),
    ("wgrad", 19.0, 17.0),
)


def dot_nn(left, right):
    return jnp.dot(left, right, preferred_element_type=jnp.float32)


def dot_nt(left, right):
    return lax.dot_general(
        left, right, (((1,), (1,)), ((), ())), preferred_element_type=jnp.float32
    )


def dot_tn(left, right):
    return lax.dot_general(
        left, right, (((0,), (0,)), ((), ())), preferred_element_type=jnp.float32
    )


def kernel(
    ids_ref, gates_ref, x_ref, c_ref, wg_ref, wu_ref, wd_ref,
    gt_ref, gg_ref, gu_ref, gd_ref,
    meta_own, meta_in, raw, rows, part, far, near, keep, qsend, qrecv, spread,
    term, term_in, tsend, trecv, final, ret, acc, send_sems, recv_sems,
):
    f32, bf16 = jnp.float32, jnp.bfloat16
    ep = lax.axis_index("ep")
    fs = lax.axis_index("fsdp")
    z, yl, co = ep // 4, (ep // 2) % 2, ep % 2
    yh, x = fs // 4, fs % 4
    xp, xm, xo = (x + 1) % 4, (x + 3) % 4, (x + 2) % 4

    def device(plane, ylo, core):
        return (plane * 4 + ylo * 2 + core, fs)

    def ring(step):
        return device((z + step + 8) % 8, yl, co)

    sibling = device(z, yl, 1 - co)
    across = device(z, 1 - yl, co)
    right, left = (ep, yh * 4 + xp), (ep, yh * 4 + xm)
    partner = (ep, (1 - yh) * 4 + x)
    mine, twin = yl * 2 + co, yl * 2 + (1 - co)
    other, other_twin = (1 - yl) * 2 + co, (1 - yl) * 2 + (1 - co)

    places = {}
    started = []

    def copy(name, source, target, where):
        place = places.setdefault(name, len(places))
        return pltpu.make_async_remote_copy(
            src_ref=source,
            dst_ref=target,
            send_sem=send_sems.at[place],
            recv_sem=recv_sems.at[place],
            device_id=where,
            device_id_type=MESH,
        )

    def start(name, source, target, where):
        made = copy(name, source, target, where)
        made.start()
        started.append(made)

    def arrive(name, target):
        copy(name, target, target, sibling).wait_recv()

    barrier = pltpu.get_barrier_semaphore()
    greeted = [ring(step) for step in range(1, 8)] + [sibling, across, right, left, partner]
    for where in greeted:
        pl.semaphore_signal(barrier, inc=1, device_id=where, device_id_type=MESH)
    pl.semaphore_wait(barrier, len(greeted))

    parts = (x_ref, c_ref)
    for p in range(2):
        start(("up", p, 1), parts[p], raw.at[0, p], ring(1))
        start(("down", p, 1), parts[p], raw.at[1, p], ring(-1))

    expert = lax.broadcasted_iota(jnp.int32, (EXPERTS, TOK), 0)
    first, second = ids_ref[0:1, :] == expert, ids_ref[1:2, :] == expert
    member = first | second
    ordered = (
        lax.broadcasted_iota(jnp.int32, (TOK, TOK), 0)
        < lax.broadcasted_iota(jnp.int32, (TOK, TOK), 1)
    )
    before = dot_nn(
        jnp.where(member, 1.0, 0.0).astype(bf16), jnp.where(ordered, 1.0, 0.0).astype(bf16)
    )
    slot = jnp.where(member, before, -1.0)
    gate = jnp.where(first, gates_ref[0:1, :], 0.0) + jnp.where(second, gates_ref[1:2, :], 0.0)
    meta_own[...] = jnp.zeros_like(meta_own)
    for e in range(EXPERTS):
        meta_own[e, 0:1, :] = slot[e : e + 1, :]
        meta_own[e, 1:2, :] = gate[e : e + 1, :]
    for i in range(1, 8):
        plane = (z - SHIFT[i] + 8) % 8
        start(("meta", i), meta_own.at[plane], meta_in.at[i], device(plane, yl, co))
    meta_in[0] = meta_own[z]
    acc[...] = jnp.zeros_like(acc)

    def onehot(slots):
        return slots == lax.broadcasted_iota(jnp.int32, (CAP, TOK), 0).astype(f32)

    def choose(i, p):
        hot = onehot(meta_in[i, 0:1, :])
        block = parts[p][...] if i == 0 else raw[i - 1, p]
        picked = dot_nn(jnp.where(hot, 1.0, 0.0).astype(bf16), block)
        if p == 1:
            weight = jnp.sum(jnp.where(hot, meta_in[i, 1:2, :], 0.0), axis=1, keepdims=True)
            picked = weight * picked
        rows[p, i, mine] = picked.astype(bf16)

    def blocks(k):
        return pl.ds(CHUNKS[k][0], CHUNKS[k][1])

    def each(k):
        return range(CHUNKS[k][0], CHUNKS[k][0] + CHUNKS[k][1])

    def take(k, p):
        if 1 <= k <= 3:
            arrive(("up", p, k), raw.at[2 * k - 2, p])
            if k < 3:
                start(("up", p, k + 1), raw.at[2 * k - 2, p], raw.at[2 * k, p], ring(1))
            elif p == 0:
                start(("far", 0), raw.at[4, 0], raw.at[6, 0], ring(1))
            arrive(("down", p, k), raw.at[2 * k - 1, p])
            if k < 3:
                start(("down", p, k + 1), raw.at[2 * k - 1, p], raw.at[2 * k + 1, p], ring(-1))
            elif p == 1:
                start(("far", 1), raw.at[5, 1], raw.at[6, 1], ring(-1))
        if k == 4:
            arrive(("far", p), raw.at[6, p])
        for i in each(k):
            if p == 0 and i > 0:
                arrive(("meta", i), meta_in.at[i])
            choose(i, p)
        own = rows.at[p, blocks(k), mine]
        start(("across", p, k), own, own, across)
        start(("twin", p, k), own, own, sibling)

    def pass_on(k, p):
        got = rows.at[p, blocks(k), other]
        arrive(("across", p, k), got)
        start(("forward", p, k), got, got, sibling)

    def complete(k, p):
        arrive(("twin", p, k), rows.at[p, blocks(k), twin])
        arrive(("forward", p, k), rows.at[p, blocks(k), other_twin])

    def put(i, at, value):
        part[:, :, i, :, at : at + HID] = value.astype(bf16).reshape(2, 4, 32, HID)

    def multiply_x(k):
        complete(k, 0)
        for i in each(k):
            block = rows[0, i].reshape(4 * CAP, FEAT)
            put(i, 0, dot_nn(block, wg_ref[...]))
            put(i, HID, dot_nn(block, wu_ref[...]))

    def multiply_c(k):
        complete(k, 1)
        for i in each(k):
            put(i, 2 * HID, dot_nn(rows[1, i].reshape(4 * CAP, FEAT), wd_ref[...]))
        at = blocks(k)
        start(("far+", k), part.at[0, xo, at], far.at[0, at], right)
        start(("far-", k), part.at[1, xo, at], far.at[1, at], left)
        start(("own+", k), part.at[1, xp, at], near.at[0, 1, at], right)
        start(("own-", k), part.at[0, xm, at], near.at[1, 0, at], left)

    def sum_far(k):
        at = blocks(k)
        arrive(("far+", k), far.at[0, at])
        part[0, xp, at] = (part[0, xp, at].astype(f32) + far[0, at].astype(f32)).astype(bf16)
        start(("sum+", k), part.at[0, xp, at], near.at[0, 0, at], right)
        arrive(("far-", k), far.at[1, at])
        part[1, xm, at] = (part[1, xm, at].astype(f32) + far[1, at].astype(f32)).astype(bf16)
        start(("sum-", k), part.at[1, xm, at], near.at[1, 1, at], left)

    def sum_near(k):
        at = blocks(k)
        arrive(("own+", k), near.at[0, 1, at])
        arrive(("own-", k), near.at[1, 0, at])
        arrive(("sum+", k), near.at[0, 0, at])
        arrive(("sum-", k), near.at[1, 1, at])

        def total(half):
            return (
                part[half, x, at].astype(f32)
                + near[0, half, at].astype(f32)
                + near[1, half, at].astype(f32)
            )

        qsend[at] = total(1 - yh).astype(bf16)
        start(("q", k), qsend.at[at], qrecv.at[at], partner)
        keep[at] = total(yh)

    def activate(k):
        at = blocks(k)
        arrive(("q", k), qrecv.at[at])
        total = keep[at] + qrecv[at].astype(f32)
        a, u, g = total[:, :, :HID], total[:, :, HID : 2 * HID], total[:, :, 2 * HID :]
        sig = jax.nn.sigmoid(a)
        silu = a * sig
        spread[yh, x, at, :, 0:HID] = (silu * u).astype(bf16)
        spread[yh, x, at, :, HID : 2 * HID] = (g * u * sig * (1.0 + a * (1.0 - sig))).astype(bf16)
        spread[yh, x, at, :, 2 * HID : 3 * HID] = (g * silu).astype(bf16)
        own = spread.at[yh, x, at]
        start(("mate", k), own, own, partner)
        start(("one+", k), own, own, right)
        start(("one-", k), own, own, left)

    def share(k):
        got = spread.at[1 - yh, x, blocks(k)]
        arrive(("mate", k), got)
        start(("two+", k), got, got, right)
        start(("two-", k), got, got, left)

    def relay(k):
        at = blocks(k)
        arrive(("one+", k), spread.at[yh, xm, at])
        arrive(("two+", k), spread.at[1 - yh, xm, at])
        start(("on+", k), spread.at[0, xm, at], spread.at[0, xm, at], right)
        arrive(("one-", k), spread.at[yh, xp, at])
        arrive(("two-", k), spread.at[1 - yh, xp, at])
        start(("on-", k), spread.at[1, xp, at], spread.at[1, xp, at], left)

    def row_terms(k):
        at = blocks(k)
        arrive(("on+", k), spread.at[0, xo, at])
        arrive(("on-", k), spread.at[1, xo, at])
        for i in each(k):
            held = spread[:, :, i].reshape(4 * CAP, 3 * HID)
            value = dot_nt(held[:, HID : 2 * HID], wg_ref[...])
            value = value + dot_nt(held[:, 2 * HID :], wu_ref[...])
            value = value.astype(bf16).reshape(2, 2, CAP, FEAT)
            term[0, i] = value[:, 0]
            term[1, i] = value[:, 1]
        start(("core", k), term.at[1 - co, at], term_in.at[at], sibling)

    def pair(k):
        at = blocks(k)
        arrive(("core", k), term_in.at[at])
        tsend[at] = (
            term[co, at, 1 - yl].astype(f32) + term_in[at, 1 - yl].astype(f32)
        ).astype(bf16)
        start(("ypair", k), tsend.at[at], trecv.at[at], across)

    def back(k):
        at = blocks(k)
        arrive(("ypair", k), trecv.at[at])
        value = (
            term[co, at, yl].astype(f32)
            + term_in[at, yl].astype(f32)
            + trecv[at].astype(f32)
        ).astype(bf16)
        if k == 0:
            ret[0] = value[0]
            return
        final[at] = value
        for i in each(k):
            home = SHIFT.index(-SHIFT[i]) if i < 7 else 7
            start(("ret", home), final.at[i], ret.at[home], ring(SHIFT[i]))

    def weight_grads(k):
        for i in each(k):
            held = spread[:, :, i].reshape(4 * CAP, 3 * HID)
            block = rows[0, i].reshape(4 * CAP, FEAT)
            acc[0] += dot_tn(held[:, HID : 2 * HID], block)
            acc[1] += dot_tn(held[:, 2 * HID :], block)
            acc[2] += dot_tn(held[:, :HID], rows[1, i].reshape(4 * CAP, FEAT))

    run = {
        "zx": lambda k: take(k, 0),
        "zc": lambda k: take(k, 1),
        "yx": lambda k: pass_on(k, 0),
        "yc": lambda k: pass_on(k, 1),
        "mx": multiply_x,
        "mc": multiply_c,
        "sum_far": sum_far,
        "sum_near": sum_near,
        "act": activate,
        "spread": share,
        "relay": relay,
        "rows": row_terms,
        "pair": pair,
        "back": back,
        "wgrad": weight_grads,
    }
    plan = []
    for k in range(len(CHUNKS)):
        for place, (name, fixed, each_block) in enumerate(STEPS):
            plan.append((ARRIVAL[k] + fixed + each_block * CHUNKS[k][1], place, k, name))
    for _, _, k, name in sorted(plan):
        run[name](k)

    gg_ref[...] = acc[0].T.astype(bf16)
    gu_ref[...] = acc[1].T.astype(bf16)
    gd_ref[...] = acc[2].T.astype(bf16)
    hots = []
    for i in range(8):
        if i > 0:
            arrive(("ret", i), ret.at[i])
        slots = meta_own[(z + SHIFT[i] + 8) % 8, 0:1, :]
        hots.append(jnp.where(onehot(slots), 1.0, 0.0).astype(bf16))
    gt_ref[...] = dot_tn(
        jnp.concatenate(hots, axis=0), ret[...].reshape(8 * CAP, FEAT)
    ).astype(bf16)
    for made in started:
        made.wait_send()


def body(tokens, cotangent, route_gates, expert_ids, w_gate, w_up, w_down):
    bf16, f32 = jnp.bfloat16, jnp.float32
    vmem = pl.BlockSpec(memory_space=pltpu.VMEM)
    shape = jax.ShapeDtypeStruct
    return pl.pallas_call(
        kernel,
        out_shape=(
            shape((TOK, FEAT), bf16),
            shape((FEAT, HID), bf16),
            shape((FEAT, HID), bf16),
            shape((FEAT, HID), bf16),
        ),
        in_specs=[vmem] * 7,
        out_specs=(vmem,) * 4,
        scratch_shapes=[
            pltpu.VMEM((EXPERTS, 8, TOK), f32),
            pltpu.VMEM((8, 8, TOK), f32),
            pltpu.VMEM((7, 2, TOK, FEAT), bf16),
            pltpu.VMEM((2, 8, 4, CAP, FEAT), bf16),
            pltpu.VMEM((2, 4, 8, 32, 3 * HID), bf16),
            pltpu.VMEM((2, 8, 32, 3 * HID), bf16),
            pltpu.VMEM((2, 2, 8, 32, 3 * HID), bf16),
            pltpu.VMEM((8, 32, 3 * HID), f32),
            pltpu.VMEM((8, 32, 3 * HID), bf16),
            pltpu.VMEM((8, 32, 3 * HID), bf16),
            pltpu.VMEM((2, 4, 8, 32, 3 * HID), bf16),
            pltpu.VMEM((2, 8, 2, CAP, FEAT), bf16),
            pltpu.VMEM((8, 2, CAP, FEAT), bf16),
            pltpu.VMEM((8, CAP, FEAT), bf16),
            pltpu.VMEM((8, CAP, FEAT), bf16),
            pltpu.VMEM((8, CAP, FEAT), bf16),
            pltpu.VMEM((8, CAP, FEAT), bf16),
            pltpu.VMEM((3, HID, FEAT), f32),
            pltpu.SemaphoreType.DMA((SEMS,)),
            pltpu.SemaphoreType.DMA((SEMS,)),
        ],
        compiler_params=pltpu.CompilerParams(
            collective_id=0, has_side_effects=True, vmem_limit_bytes=60 * 1024 * 1024
        ),
    )(expert_ids.T, route_gates.T, tokens, cotangent, w_gate, w_up, w_down)


def solution(mesh):
    placed = (
        P("ep", "fsdp"),
        P("ep", "fsdp"),
        P("ep", None),
        P("ep", None),
        P("fsdp", "ep"),
        P("fsdp", "ep"),
        P("fsdp", "ep"),
    )
    return jax.shard_map(
        body,
        mesh=mesh,
        in_specs=placed,
        out_specs=(P("ep", "fsdp"), P("fsdp", "ep"), P("fsdp", "ep"), P("fsdp", "ep")),
        check_vma=False,
    )
```

time: 462 us -> 149 us (0.32)
  waiting for transfers between devices: 225 us -> 0 us
  blocking collectives: 174 us -> 0 us
  Pallas kernels: 0 us -> 141 us
  matrix products: 23.4 us -> 0 us
  between operations: 14.2 us -> 0.65 us
  other arithmetic: 9.36 us -> 0 us
  starting transfers between devices: 8.1 us -> 0 us
    all_to_all x1 -> x0, blocking collectives: 174 us -> none  [body(): lax.all_to_all(outgoing.reshape(2, ep_count, CAP, width), 'ep', split_axi...]
    psum x1 -> x0, waiting for transfers between devices: 149 us -> none  [body(): lax.psum((jnp.dot(rows_x, w_gate, preferred_element_type=jnp.float32), jn...]
    pallas_call x0 -> x1, Pallas kernels: none -> 141 us  [body(): pl.pallas_call(kernel, out_shape=(shape((TOK, FEAT), bf16), shape((FEAT,...]
    all_to_all x1 -> x0, waiting for transfers between devices: 75.4 us -> none  [body(): lax.all_to_all(row_term.reshape(ep_count, CAP, width), 'ep', split_axis=0...]
    dot_general x12 -> x0, matrix products: 23.4 us -> none  [the longest x3 8.17 us: cross_dot(): lax.dot_general(left, right, (((0,), (0,)), ((), ())), preferred_element_...]
    all_to_all x1 -> x0, starting transfers between devices: 8.06 us -> none  [body(): lax.all_to_all(row_term.reshape(ep_count, CAP, width), 'ep', split_axis=0...]
    reduce_sum x3 -> x0, other arithmetic: 4.71 us -> none  [the longest x1 2.75 us: body(): jnp.sum(returned.reshape(EXPERTS, split_ways, CAP, width).astype(jnp.floa...]
  transfers between devices with their start and end apart: 2 -> 0, of which waited for: 2 -> 0; matrix products, arithmetic and copies ran while one was open for 2% -> 0% of each run, Pallas kernels for 0% -> 0%
where the time goes in v1:
time: 149 us; the launch traced here: 147 us
  Pallas kernels  141 us (95%)
  local copies, waits for them, and re-layouts  4.84 us (3%)
    pallas_call x1, Pallas kernels, body(): pl.pallas_call(kernel, out_shape=(shape((TOK, FEAT), bf16), shape((FEAT,...  141 us
    unnamed x10, local copies, waits for them, and re-layouts  4.84 us

profile of v1, /device:TPU:1, one launch (start us, length us, event | category | flops | bytes accessed | tf_op | source)
XLA Modules:
  0.0 146.9 jit_solution(14779441737174148348)
XLA Ops:
  0.6 141.4 %shard_map.102 = (bf16[128,896]{1,0:T(8,128)(2,1)}, bf16[896,256]{1,0:T(8,128)(2,1)}, bf16[896,256]{1,0:T(8,128)(2,1)}, bf16[896,256]{1,0:T(8,128)(2,1)}) custom-call(s32[2,128]{1,0:T(2,128)} %bitcast.2, f32[2,128]{1,0:T(2,128)} %bitcast.3, bf16[128,896]{1,0:T(8,128)(2,1)} %x_ref.1, bf16[128,896]{1,0:T(8,128)(2,1)} %c_ref.1, bf16[896,256]{1,0:T(8,128)(2,1)} %wg_ref.1, ...), custom_call_target="tpu_custom_call" | custom-call | tf_op jit(solution)/shard_map/pallas_call | solution.py:351
  142.0 0.0 copy-start.2
  142.0 1.7 %copy.15 = bf16[128,896]{1,0:T(8,128)(2,1)} copy(bf16[128,896]{1,0:T(8,128)(2,1)} %get-tuple-element.8) | data formatting | bytes 458752
  143.7 0.0 copy-done.2
  143.7 0.0 copy-start.1
  143.7 0.8 copy.16
  144.5 0.4 copy-done.1
  144.9 0.0 copy-start
  144.9 0.8 copy.17
  145.7 0.4 copy-done
  146.1 0.8 copy.18
Async XLA Ops:
  142.0 1.7 %copy-start.2 = (bf16[896,256]{1,0:T(8,128)(2,1)S(1)}, bf16[896,256]{1,0:T(8,128)(2,1)}, u32[]{:S(2)}) copy-start(bf16[896,256]{1,0:T(8,128)(2,1)} %get-tuple-element.9) | copy-start | bytes 1376260
  143.7 1.2 copy-start.1
  144.9 1.2 copy-start

commit v2 on v1

v2 whole, which is shorter than its diff:
```python
import jax
import jax.numpy as jnp
from jax import lax
from jax.experimental import pallas as pl
from jax.experimental.pallas import tpu as pltpu
from jax.sharding import PartitionSpec as P

EXPERTS = 8
CAP = 64
TOK = 128
FEAT = 896
HID = 256
MESH = pl.DeviceIdType.MESH

SHIFT = (0, -1, 1, -2, 2, -3, 3, 4)
BLOCKS = 8
SEMS = 288

ORDER = (
    0, 8, 1, 2, 10, 17, 9, 16, 18, 4, 26, 34, 3, 42, 25, 33,
    41, 11, 24, 32, 40, 12, 5, 6, 19, 20, 27, 49, 50, 28, 35, 43,
    36, 14, 48, 21, 44, 13, 7, 51, 22, 52, 30, 37, 38, 46, 59, 29,
    15, 54, 23, 45, 67, 56, 62, 60, 53, 31, 39, 47, 75, 61, 70, 55,
    58, 57, 83, 78, 69, 68, 63, 91, 86, 77, 65, 99, 94, 76, 85, 71,
    102, 84, 66, 118, 93, 117, 64, 79, 107, 73, 110, 101, 92, 100, 87, 74,
    109, 81, 95, 72, 108, 82, 103, 89, 97, 80, 90, 111, 114, 98, 88, 112,
    113, 105, 96, 119, 106, 115, 104, 116,
)


def dot_nn(left, right):
    return jnp.dot(left, right, preferred_element_type=jnp.float32)


def dot_nt(left, right):
    return lax.dot_general(
        left, right, (((1,), (1,)), ((), ())), preferred_element_type=jnp.float32
    )


def dot_tn(left, right):
    return lax.dot_general(
        left, right, (((0,), (0,)), ((), ())), preferred_element_type=jnp.float32
    )


def kernel(
    ids_ref, gates_ref, x_ref, c_ref, wg_ref, wu_ref, wd_ref,
    gt_ref, gg_ref, gu_ref, gd_ref,
    meta_own, meta_in, meta_far, raw, rows, far_rows, own, part, far, near,
    keep, qsend, qrecv, spread, term, kept, term_in, tsend, trecv, final, ret, acc,
    send_sems, recv_sems,
):
    f32, bf16 = jnp.float32, jnp.bfloat16
    ep = lax.axis_index("ep")
    fs = lax.axis_index("fsdp")
    z, yl, co = ep // 4, (ep // 2) % 2, ep % 2
    yh, x = fs // 4, fs % 4
    xp, xm, xo = (x + 1) % 4, (x + 3) % 4, (x + 2) % 4

    def device(plane, ylo, core):
        return (plane * 4 + ylo * 2 + core, fs)

    def ring(step):
        return device((z + step + 8) % 8, yl, co)

    sibling = device(z, yl, 1 - co)
    across = device(z, 1 - yl, co)
    right, left = (ep, yh * 4 + xp), (ep, yh * 4 + xm)
    partner = (ep, (1 - yh) * 4 + x)
    mine, twin = yl * 2 + co, yl * 2 + (1 - co)
    other, other_twin = (1 - yl) * 2 + co, (1 - yl) * 2 + (1 - co)

    places = {}
    started = []

    def copy(name, source, target, where):
        place = places.setdefault(name, len(places))
        return pltpu.make_async_remote_copy(
            src_ref=source,
            dst_ref=target,
            send_sem=send_sems.at[place],
            recv_sem=recv_sems.at[place],
            device_id=where,
            device_id_type=MESH,
        )

    def start(name, source, target, where):
        made = copy(name, source, target, where)
        made.start()
        started.append(made)

    def arrive(name, target):
        copy(name, target, target, sibling).wait_recv()

    barrier = pltpu.get_barrier_semaphore()
    greeted = [ring(step) for step in range(1, 8)] + [sibling, across, right, left, partner]
    for where in greeted:
        pl.semaphore_signal(barrier, inc=1, device_id=where, device_id_type=MESH)
    pl.semaphore_wait(barrier, len(greeted))

    parts = (x_ref, c_ref)
    for p in range(2):
        start(("up", p, 1), parts[p], raw.at[0, p], ring(1))
        start(("down", p, 2), parts[p], raw.at[1, p], ring(-1))

    expert = lax.broadcasted_iota(jnp.int32, (EXPERTS, TOK), 0)
    first, second = ids_ref[0:1, :] == expert, ids_ref[1:2, :] == expert
    member = first | second
    ordered = (
        lax.broadcasted_iota(jnp.int32, (TOK, TOK), 0)
        < lax.broadcasted_iota(jnp.int32, (TOK, TOK), 1)
    )
    before = dot_nn(
        jnp.where(member, 1.0, 0.0).astype(bf16), jnp.where(ordered, 1.0, 0.0).astype(bf16)
    )
    slot = jnp.where(member, before, -1.0)
    gate = jnp.where(first, gates_ref[0:1, :], 0.0) + jnp.where(second, gates_ref[1:2, :], 0.0)
    meta_own[...] = jnp.zeros_like(meta_own)
    for e in range(EXPERTS):
        meta_own[e, 0:1, :] = slot[e : e + 1, :]
        meta_own[e, 1:2, :] = gate[e : e + 1, :]
    for i in range(1, 7):
        plane = (z - SHIFT[i] + 8) % 8
        start(("meta", i), meta_own.at[plane], meta_in.at[i], device(plane, yl, co))
    facing = meta_own.at[(z + 4) % 8]
    start(("meta", 8), facing, meta_far.at[0], ring(3))
    start(("meta", 9), facing, meta_far.at[1], ring(-3))
    meta_in[0] = meta_own[z]
    acc[...] = jnp.zeros_like(acc)

    def onehot(slots):
        return slots == lax.broadcasted_iota(jnp.int32, (CAP, TOK), 0).astype(f32)

    def choose(block, meta, p):
        hot = onehot(meta[0:1, :])
        picked = dot_nn(jnp.where(hot, 1.0, 0.0).astype(bf16), block)
        if p == 1:
            weight = jnp.sum(jnp.where(hot, meta[1:2, :], 0.0), axis=1, keepdims=True)
            picked = weight * picked
        return picked.astype(bf16)

    def take(i, p):
        if 1 <= i <= 6:
            name, away = ("up", 1) if i % 2 else ("down", -1)
            got = raw.at[i - 1, p]
            arrive((name, p, i), got)
            if i < 5:
                start((name, p, i + 2), got, raw.at[i + 1, p], ring(away))
            elif p == i - 5:
                arrive(("meta", 8 + p), meta_far.at[p])
                far_rows[p] = choose(raw[i - 1, p], meta_far[p], p)
                start(("last", p), far_rows.at[p], rows.at[p, 7, mine], ring(away))
        if i == 7:
            arrive(("last", p), rows.at[p, 7, mine])
        else:
            if p == 0 and i > 0:
                arrive(("meta", i), meta_in.at[i])
            block = parts[p][...] if i == 0 else raw[i - 1, p]
            rows[p, i, mine] = choose(block, meta_in[i], p)
        chosen = rows.at[p, i, mine]
        start(("across", p, i), chosen, chosen, across)
        start(("twin", p, i), chosen, chosen, sibling)

    def pass_on(i, p):
        got = rows.at[p, i, other]
        arrive(("across", p, i), got)
        start(("forward", p, i), got, got, sibling)

    def complete(i, p):
        arrive(("twin", p, i), rows.at[p, i, twin])
        arrive(("forward", p, i), rows.at[p, i, other_twin])

    def put(i, at, value):
        value = value.reshape(2, 4, 32, HID)
        own[:, :, i, :, at : at + HID] = value
        part[:, :, i, :, at : at + HID] = value.astype(bf16)

    def multiply_x(i):
        complete(i, 0)
        block = rows[0, i].reshape(4 * CAP, FEAT)
        put(i, 0, dot_nn(block, wg_ref[...]))
        put(i, HID, dot_nn(block, wu_ref[...]))

    def multiply_c(i):
        complete(i, 1)
        put(i, 2 * HID, dot_nn(rows[1, i].reshape(4 * CAP, FEAT), wd_ref[...]))
        start(("far+", i), part.at[0, xo, i], far.at[0, i], right)
        start(("far-", i), part.at[1, xo, i], far.at[1, i], left)
        start(("own+", i), part.at[1, xp, i], near.at[0, 1, i], right)
        start(("own-", i), part.at[0, xm, i], near.at[1, 0, i], left)

    def sum_far(i):
        arrive(("far+", i), far.at[0, i])
        part[0, xp, i] = (own[0, xp, i] + far[0, i].astype(f32)).astype(bf16)
        start(("sum+", i), part.at[0, xp, i], near.at[0, 0, i], right)
        arrive(("far-", i), far.at[1, i])
        part[1, xm, i] = (own[1, xm, i] + far[1, i].astype(f32)).astype(bf16)
        start(("sum-", i), part.at[1, xm, i], near.at[1, 1, i], left)

    def sum_near(i):
        arrive(("own+", i), near.at[0, 1, i])
        arrive(("own-", i), near.at[1, 0, i])
        arrive(("sum+", i), near.at[0, 0, i])
        arrive(("sum-", i), near.at[1, 1, i])

        def total(half):
            return own[half, x, i] + near[0, half, i].astype(f32) + near[1, half, i].astype(f32)

        qsend[i] = total(1 - yh).astype(bf16)
        start(("q", i), qsend.at[i], qrecv.at[i], partner)
        keep[i] = total(yh)

    def activate(i):
        arrive(("q", i), qrecv.at[i])
        total = keep[i] + qrecv[i].astype(f32)
        a, u, g = total[:, :HID], total[:, HID : 2 * HID], total[:, 2 * HID :]
        sig = jax.nn.sigmoid(a)
        silu = a * sig
        spread[yh, x, i, :, 0:HID] = (silu * u).astype(bf16)
        spread[yh, x, i, :, HID : 2 * HID] = (g * u * sig * (1.0 + a * (1.0 - sig))).astype(bf16)
        spread[yh, x, i, :, 2 * HID : 3 * HID] = (g * silu).astype(bf16)
        made = spread.at[yh, x, i]
        start(("mate", i), made, made, partner)
        start(("one+", i), made, made, right)
        start(("one-", i), made, made, left)

    def share(i):
        got = spread.at[1 - yh, x, i]
        arrive(("mate", i), got)
        start(("two+", i), got, got, right)
        start(("two-", i), got, got, left)

    def relay(i):
        arrive(("one+", i), spread.at[yh, xm, i])
        arrive(("two+", i), spread.at[1 - yh, xm, i])
        start(("on+", i), spread.at[0, xm, i], spread.at[0, xm, i], right)
        arrive(("one-", i), spread.at[yh, xp, i])
        arrive(("two-", i), spread.at[1 - yh, xp, i])
        start(("on-", i), spread.at[1, xp, i], spread.at[1, xp, i], left)

    def row_terms(i):
        arrive(("on+", i), spread.at[0, xo, i])
        arrive(("on-", i), spread.at[1, xo, i])

        def product(core):
            held = spread[:, pl.ds(2 * core, 2), i].reshape(2 * CAP, 3 * HID)
            value = dot_nt(held[:, HID : 2 * HID], wg_ref[...])
            value = value + dot_nt(held[:, 2 * HID :], wu_ref[...])
            return value.reshape(2, CAP, FEAT)

        term[i] = product(1 - co).astype(bf16)
        start(("core", i), term.at[i], term_in.at[i], sibling)
        kept[i] = product(co)

    def pair(i):
        arrive(("core", i), term_in.at[i])
        tsend[i] = (kept[i, 1 - yl] + term_in[i, 1 - yl].astype(f32)).astype(bf16)
        start(("ypair", i), tsend.at[i], trecv.at[i], across)

    def back(i):
        arrive(("ypair", i), trecv.at[i])
        value = kept[i, yl] + term_in[i, yl].astype(f32) + trecv[i].astype(f32)
        if i == 0:
            ret[0] = value.astype(bf16)
            return
        final[i] = value.astype(bf16)
        home = SHIFT.index(-SHIFT[i]) if i < 7 else 7
        start(("ret", home), final.at[i], ret.at[home], ring(SHIFT[i]))

    def weight_grads(i):
        held = spread[:, :, i].reshape(4 * CAP, 3 * HID)
        block = rows[0, i].reshape(4 * CAP, FEAT)
        acc[0] += dot_tn(held[:, HID : 2 * HID], block)
        acc[1] += dot_tn(held[:, 2 * HID :], block)
        acc[2] += dot_tn(held[:, :HID], rows[1, i].reshape(4 * CAP, FEAT))

    run = (
        lambda i: take(i, 0),
        lambda i: take(i, 1),
        lambda i: pass_on(i, 0),
        lambda i: pass_on(i, 1),
        multiply_x,
        multiply_c,
        sum_far,
        sum_near,
        activate,
        share,
        relay,
        row_terms,
        pair,
        back,
        weight_grads,
    )
    for item in ORDER:
        run[item // BLOCKS](item % BLOCKS)

    gg_ref[...] = acc[0].T.astype(bf16)
    gu_ref[...] = acc[1].T.astype(bf16)
    gd_ref[...] = acc[2].T.astype(bf16)
    hots = []
    for i in range(8):
        if i > 0:
            arrive(("ret", i), ret.at[i])
        slots = meta_own[(z + SHIFT[i] + 8) % 8, 0:1, :]
        hots.append(jnp.where(onehot(slots), 1.0, 0.0).astype(bf16))
    gt_ref[...] = dot_tn(
        jnp.concatenate(hots, axis=0), ret[...].reshape(8 * CAP, FEAT)
    ).astype(bf16)
    for made in started:
        made.wait_send()


def body(tokens, cotangent, route_gates, expert_ids, w_gate, w_up, w_down):
    bf16, f32 = jnp.bfloat16, jnp.float32
    vmem = pl.BlockSpec(memory_space=pltpu.VMEM)
    shape = jax.ShapeDtypeStruct
    return pl.pallas_call(
        kernel,
        out_shape=(
            shape((TOK, FEAT), bf16),
            shape((FEAT, HID), bf16),
            shape((FEAT, HID), bf16),
            shape((FEAT, HID), bf16),
        ),
        in_specs=[vmem] * 7,
        out_specs=(vmem,) * 4,
        scratch_shapes=[
            pltpu.VMEM((EXPERTS, 8, TOK), f32),
            pltpu.VMEM((8, 8, TOK), f32),
            pltpu.VMEM((2, 8, TOK), f32),
            pltpu.VMEM((6, 2, TOK, FEAT), bf16),
            pltpu.VMEM((2, 8, 4, CAP, FEAT), bf16),
            pltpu.VMEM((2, CAP, FEAT), bf16),
            pltpu.VMEM((2, 4, 8, 32, 3 * HID), f32),
            pltpu.VMEM((2, 4, 8, 32, 3 * HID), bf16),
            pltpu.VMEM((2, 8, 32, 3 * HID), bf16),
            pltpu.VMEM((2, 2, 8, 32, 3 * HID), bf16),
            pltpu.VMEM((8, 32, 3 * HID), f32),
            pltpu.VMEM((8, 32, 3 * HID), bf16),
            pltpu.VMEM((8, 32, 3 * HID), bf16),
            pltpu.VMEM((2, 4, 8, 32, 3 * HID), bf16),
            pltpu.VMEM((8, 2, CAP, FEAT), bf16),
            pltpu.VMEM((8, 2, CAP, FEAT), f32),
            pltpu.VMEM((8, 2, CAP, FEAT), bf16),
            pltpu.VMEM((8, CAP, FEAT), bf16),
            pltpu.VMEM((8, CAP, FEAT), bf16),
            pltpu.VMEM((8, CAP, FEAT), bf16),
            pltpu.VMEM((8, CAP, FEAT), bf16),
            pltpu.VMEM((3, HID, FEAT), f32),
            pltpu.SemaphoreType.DMA((SEMS,)),
            pltpu.SemaphoreType.DMA((SEMS,)),
        ],
        compiler_params=pltpu.CompilerParams(
            collective_id=0, has_side_effects=True, vmem_limit_bytes=60 * 1024 * 1024
        ),
    )(expert_ids.T, route_gates.T, tokens, cotangent, w_gate, w_up, w_down)


def solution(mesh):
    placed = (
        P("ep", "fsdp"),
        P("ep", "fsdp"),
        P("ep", None),
        P("ep", None),
        P("fsdp", "ep"),
        P("fsdp", "ep"),
        P("fsdp", "ep"),
    )
    return jax.shard_map(
        body,
        mesh=mesh,
        in_specs=placed,
        out_specs=(P("ep", "fsdp"), P("fsdp", "ep"), P("fsdp", "ep"), P("fsdp", "ep")),
        check_vma=False,
    )
```

time: 149 us -> 125 us (0.84); the launches traced: 147 us -> 124 us
  Pallas kernels: 141 us -> 119 us
    pallas_call x1, Pallas kernels: 141 us -> 119 us  [body(): pl.pallas_call(kernel, out_shape=(shape((TOK, FEAT), bf16), shape((FEAT,...]
where the time goes in v2:
time: 125 us; the launch traced here: 124 us
  Pallas kernels  119 us (95%)
  local copies, waits for them, and re-layouts  4.84 us (4%)
    pallas_call x1, Pallas kernels, body(): pl.pallas_call(kernel, out_shape=(shape((TOK, FEAT), bf16), shape((FEAT,...  119 us
    unnamed x10, local copies, waits for them, and re-layouts  4.84 us

profile of v2, /device:TPU:1, one launch (start us, length us, event | category | flops | bytes accessed | tf_op | source)
XLA Modules:
  0.0 124.5 jit_solution(16739419099971825705)
XLA Ops:
  0.6 119.0 %shard_map.102 = (bf16[128,896]{1,0:T(8,128)(2,1)}, bf16[896,256]{1,0:T(8,128)(2,1)}, bf16[896,256]{1,0:T(8,128)(2,1)}, bf16[896,256]{1,0:T(8,128)(2,1)}) custom-call(s32[2,128]{1,0:T(2,128)} %bitcast.2, f32[2,128]{1,0:T(2,128)} %bitcast.3, bf16[128,896]{1,0:T(8,128)(2,1)} %x_ref.1, bf16[128,896]{1,0:T(8,128)(2,1)} %c_ref.1, bf16[896,256]{1,0:T(8,128)(2,1)} %wg_ref.1, ...), custom_call_target="tpu_custom_call" | custom-call | tf_op jit(solution)/shard_map/pallas_call | solution.py:318
  119.6 0.0 copy-start.2
  119.6 1.7 %copy.15 = bf16[128,896]{1,0:T(8,128)(2,1)} copy(bf16[128,896]{1,0:T(8,128)(2,1)} %get-tuple-element.8) | data formatting | bytes 458752
  121.3 0.0 copy-done.2
  121.3 0.0 copy-start.1
  121.3 0.8 copy.16
  122.1 0.4 copy-done.1
  122.5 0.0 copy-start
  122.5 0.8 copy.17
  123.3 0.4 copy-done
  123.7 0.8 copy.18
Async XLA Ops:
  119.6 1.7 %copy-start.2 = (bf16[896,256]{1,0:T(8,128)(2,1)S(1)}, bf16[896,256]{1,0:T(8,128)(2,1)}, u32[]{:S(2)}) copy-start(bf16[896,256]{1,0:T(8,128)(2,1)} %get-tuple-element.9) | copy-start | bytes 1376260
  121.3 1.2 copy-start.1
  122.5 1.2 copy-start

commit v3 on v2

--- a/solution.py
+++ b/solution.py
@@ -17,14 +17,14 @@
 SEMS = 288
 
 ORDER = (
-    0, 8, 1, 2, 10, 17, 9, 16, 18, 4, 26, 34, 3, 42, 25, 33,
-    41, 11, 24, 32, 40, 12, 5, 6, 19, 20, 27, 49, 50, 28, 35, 43,
-    36, 14, 48, 21, 44, 13, 7, 51, 22, 52, 30, 37, 38, 46, 59, 29,
-    15, 54, 23, 45, 67, 56, 62, 60, 53, 31, 39, 47, 75, 61, 70, 55,
-    58, 57, 83, 78, 69, 68, 63, 91, 86, 77, 65, 99, 94, 76, 85, 71,
-    102, 84, 66, 118, 93, 117, 64, 79, 107, 73, 110, 101, 92, 100, 87, 74,
-    109, 81, 95, 72, 108, 82, 103, 89, 97, 80, 90, 111, 114, 98, 88, 112,
-    113, 105, 96, 119, 106, 115, 104, 116,
+    0, 8, 1, 2, 16, 10, 9, 4, 3, 24, 17, 32, 40, 11, 12, 26,
+    25, 33, 41, 18, 48, 6, 5, 34, 42, 19, 27, 35, 43, 20, 49, 13,
+    28, 14, 36, 44, 50, 51, 21, 22, 29, 7, 15, 38, 52, 37, 45, 30,
+    58, 46, 60, 53, 23, 31, 59, 54, 39, 47, 61, 68, 62, 55, 67, 69,
+    76, 70, 63, 57, 77, 56, 84, 78, 85, 71, 75, 66, 92, 86, 65, 100,
+    93, 83, 101, 79, 74, 73, 94, 118, 64, 116, 91, 108, 102, 87, 109, 82,
+    99, 81, 117, 72, 95, 110, 90, 119, 103, 89, 107, 113, 114, 98, 80, 97,
+    111, 88, 96, 105, 106, 104, 115, 112,
 )
 
 
@@ -45,11 +45,12 @@
 
 
 def kernel(
-    ids_ref, gates_ref, x_ref, c_ref, wg_ref, wu_ref, wd_ref,
-    gt_ref, gg_ref, gu_ref, gd_ref,
+    ids_ref, gates_ref, x_in, c_in, wg_in, wu_in, wd_in,
+    gt_out, gg_out, gu_out, gd_out,
+    x_ref, c_ref, wg_ref, wu_ref, wd_ref, gt_ref, wgrads,
     meta_own, meta_in, meta_far, raw, rows, far_rows, own, part, far, near,
     keep, qsend, qrecv, spread, term, kept, term_in, tsend, trecv, final, ret, acc,
-    send_sems, recv_sems,
+    send_sems, recv_sems, load_sems, store_sems,
 ):
     f32, bf16 = jnp.float32, jnp.bfloat16
     ep = lax.axis_index("ep")
@@ -97,12 +98,16 @@
     greeted = [ring(step) for step in range(1, 8)] + [sibling, across, right, left, partner]
     for where in greeted:
         pl.semaphore_signal(barrier, inc=1, device_id=where, device_id_type=MESH)
-    pl.semaphore_wait(barrier, len(greeted))
-
+
+    loads = [
+        pltpu.make_async_copy(source, target, load_sems.at[place])
+        for place, (source, target) in enumerate(
+            ((x_in, x_ref), (c_in, c_ref), (wg_in, wg_ref), (wu_in, wu_ref), (wd_in, wd_ref))
+        )
+    ]
+    for load in loads:
+        load.start()
     parts = (x_ref, c_ref)
-    for p in range(2):
-        start(("up", p, 1), parts[p], raw.at[0, p], ring(1))
-        start(("down", p, 2), parts[p], raw.at[1, p], ring(-1))
 
     expert = lax.broadcasted_iota(jnp.int32, (EXPERTS, TOK), 0)
     first, second = ids_ref[0:1, :] == expert, ids_ref[1:2, :] == expert
@@ -120,14 +125,20 @@
     for e in range(EXPERTS):
         meta_own[e, 0:1, :] = slot[e : e + 1, :]
         meta_own[e, 1:2, :] = gate[e : e + 1, :]
+    meta_in[0] = meta_own[z]
+    acc[...] = jnp.zeros_like(acc)
+
+    pl.semaphore_wait(barrier, len(greeted))
+    for p in range(2):
+        loads[p].wait()
+        start(("up", p, 1), parts[p], raw.at[0, p], ring(1))
+        start(("down", p, 2), parts[p], raw.at[1, p], ring(-1))
     for i in range(1, 7):
         plane = (z - SHIFT[i] + 8) % 8
         start(("meta", i), meta_own.at[plane], meta_in.at[i], device(plane, yl, co))
     facing = meta_own.at[(z + 4) % 8]
     start(("meta", 8), facing, meta_far.at[0], ring(3))
     start(("meta", 9), facing, meta_far.at[1], ring(-3))
-    meta_in[0] = meta_own[z]
-    acc[...] = jnp.zeros_like(acc)
 
     def onehot(slots):
         return slots == lax.broadcasted_iota(jnp.int32, (CAP, TOK), 0).astype(f32)
@@ -292,40 +303,59 @@
         back,
         weight_grads,
     )
+    loaded = False
     for item in ORDER:
+        if run[item // BLOCKS] is multiply_x and not loaded:
+            for load in loads[2:]:
+                load.wait()
+            loaded = True
         run[item // BLOCKS](item % BLOCKS)
 
-    gg_ref[...] = acc[0].T.astype(bf16)
-    gu_ref[...] = acc[1].T.astype(bf16)
-    gd_ref[...] = acc[2].T.astype(bf16)
+    stores = []
+    for place, target in enumerate((gg_out, gu_out, gd_out)):
+        wgrads[place] = acc[place].T.astype(bf16)
+        stores.append(pltpu.make_async_copy(wgrads.at[place], target, store_sems.at[place]))
+        stores[-1].start()
     hots = []
     for i in range(8):
-        if i > 0:
-            arrive(("ret", i), ret.at[i])
         slots = meta_own[(z + SHIFT[i] + 8) % 8, 0:1, :]
         hots.append(jnp.where(onehot(slots), 1.0, 0.0).astype(bf16))
-    gt_ref[...] = dot_tn(
-        jnp.concatenate(hots, axis=0), ret[...].reshape(8 * CAP, FEAT)
-    ).astype(bf16)
+    hots = jnp.concatenate(hots, axis=0)
     for made in started:
         made.wait_send()
+    for i in range(1, 8):
+        arrive(("ret", i), ret.at[i])
+    gt_ref[...] = dot_tn(hots, ret[...].reshape(8 * CAP, FEAT)).astype(bf16)
+    stores.append(pltpu.make_async_copy(gt_ref, gt_out, store_sems.at[3]))
+    stores[-1].start()
+    for store in stores:
+        store.wait()
+
+
+def hand_on(*refs):
+    for source, target in zip(refs[:4], refs[4:]):
+        target[...] = source[...]
 
 
 def body(tokens, cotangent, route_gates, expert_ids, w_gate, w_up, w_down):
     bf16, f32 = jnp.bfloat16, jnp.float32
     vmem = pl.BlockSpec(memory_space=pltpu.VMEM)
+    anywhere = pl.BlockSpec(memory_space=pl.ANY)
     shape = jax.ShapeDtypeStruct
-    return pl.pallas_call(
+    outs = (shape((TOK, FEAT), bf16),) + (shape((FEAT, HID), bf16),) * 3
+    results = pl.pallas_call(
         kernel,
-        out_shape=(
-            shape((TOK, FEAT), bf16),
-            shape((FEAT, HID), bf16),
-            shape((FEAT, HID), bf16),
-            shape((FEAT, HID), bf16),
-        ),
-        in_specs=[vmem] * 7,
-        out_specs=(vmem,) * 4,
+        out_shape=outs,
+        in_specs=[vmem] * 2 + [anywhere] * 5,
+        out_specs=(anywhere,) * 4,
         scratch_shapes=[
+            pltpu.VMEM((TOK, FEAT), bf16),
+            pltpu.VMEM((TOK, FEAT), bf16),
+            pltpu.VMEM((FEAT, HID), bf16),
+            pltpu.VMEM((FEAT, HID), bf16),
+            pltpu.VMEM((FEAT, HID), bf16),
+            pltpu.VMEM((TOK, FEAT), bf16),
+            pltpu.VMEM((3, FEAT, HID), bf16),
             pltpu.VMEM((EXPERTS, 8, TOK), f32),
             pltpu.VMEM((8, 8, TOK), f32),
             pltpu.VMEM((2, 8, TOK), f32),
@@ -350,11 +380,19 @@
             pltpu.VMEM((3, HID, FEAT), f32),
             pltpu.SemaphoreType.DMA((SEMS,)),
             pltpu.SemaphoreType.DMA((SEMS,)),
+            pltpu.SemaphoreType.DMA((5,)),
+            pltpu.SemaphoreType.DMA((4,)),
         ],
         compiler_params=pltpu.CompilerParams(
             collective_id=0, has_side_effects=True, vmem_limit_bytes=60 * 1024 * 1024
         ),
     )(expert_ids.T, route_gates.T, tokens, cotangent, w_gate, w_up, w_down)
+    return pl.pallas_call(
+        hand_on,
+        out_shape=outs,
+        in_specs=[vmem] * 4,
+        out_specs=(vmem,) * 4,
+    )(*results)
 
 
 def solution(mesh):

time: 125 us -> 116 us (0.928)
  local copies, waits for them, and re-layouts: 4.84 us -> 0 us
  Pallas kernels: 119 us -> 115 us
    unnamed x10 -> x0, local copies, waits for them, and re-layouts: 4.84 us -> none
    pallas_call x1 -> x2, Pallas kernels: 119 us -> 115 us  [the longest x1 112 us: body(): pl.pallas_call(kernel, out_shape=outs, in_specs=[vmem] * 2 + [anywhere] *...]
where the time goes in v3:
time: 116 us; the launch traced here: 115 us
  Pallas kernels  115 us (99%)
    pallas_call x1, Pallas kernels, body(): pl.pallas_call(kernel, out_shape=outs, in_specs=[vmem] * 2 + [anywhere] *...  112 us
    pallas_call x1, Pallas kernels, body(): pl.pallas_call(hand_on, out_shape=outs, in_specs=[vmem] * 4, out_specs=(v...  2.58 us

profile of v3, /device:TPU:1, one launch (start us, length us, event | category | flops | bytes accessed | tf_op | source)
XLA Modules:
  0.0 115.4 jit_solution(10780636859882351874)
XLA Ops:
  0.6 112.2 %shard_map.102 = (bf16[128,896]{1,0:T(8,128)(2,1)}, bf16[896,256]{1,0:T(8,128)(2,1)}, bf16[896,256]{1,0:T(8,128)(2,1)}, bf16[896,256]{1,0:T(8,128)(2,1)}) custom-call(s32[2,128]{1,0:T(2,128)} %bitcast.2, f32[2,128]{1,0:T(2,128)} %bitcast.3, bf16[128,896]{1,0:T(8,128)(2,1)} %x_in.1, bf16[128,896]{1,0:T(8,128)(2,1)} %c_in.1, bf16[896,256]{1,0:T(8,128)(2,1)} %wg_in.1, ...), custom_call_target="tpu_custom_call" | custom-call | tf_op jit(solution)/shard_map/pallas_call | solution.py:346
  112.9 2.6 %shard_map.103 = (bf16[128,896]{1,0:T(8,128)(2,1)}, bf16[896,256]{1,0:T(8,128)(2,1)}, bf16[896,256]{1,0:T(8,128)(2,1)}, bf16[896,256]{1,0:T(8,128)(2,1)}) custom-call(bf16[128,896]{1,0:T(8,128)(2,1)} %get-tuple-element.8.refs_0_, bf16[896,256]{1,0:T(8,128)(2,1)} %get-tuple-element.9.refs_1_, bf16[896,256]{1,0:T(8,128)(2,1)} %get-tuple-element.10.refs_2_, ...), custom_call_target="tpu_custom_call" | custom-call | tf_op jit(solution)/shard_map/pallas_call | solution.py:390

commit v4 on v3

--- a/solution.py
+++ b/solution.py
@@ -17,14 +17,13 @@
 SEMS = 288
 
 ORDER = (
-    0, 8, 1, 2, 16, 10, 9, 4, 3, 24, 17, 32, 40, 11, 12, 26,
-    25, 33, 41, 18, 48, 6, 5, 34, 42, 19, 27, 35, 43, 20, 49, 13,
-    28, 14, 36, 44, 50, 51, 21, 22, 29, 7, 15, 38, 52, 37, 45, 30,
-    58, 46, 60, 53, 23, 31, 59, 54, 39, 47, 61, 68, 62, 55, 67, 69,
-    76, 70, 63, 57, 77, 56, 84, 78, 85, 71, 75, 66, 92, 86, 65, 100,
-    93, 83, 101, 79, 74, 73, 94, 118, 64, 116, 91, 108, 102, 87, 109, 82,
-    99, 81, 117, 72, 95, 110, 90, 119, 103, 89, 107, 113, 114, 98, 80, 97,
-    111, 88, 96, 105, 106, 104, 115, 112,
+    0, 8, 1, 16, 2, 24, 9, 10, 32, 40, 18, 3, 4, 25, 34, 26,
+    17, 12, 42, 11, 33, 41, 6, 5, 20, 28, 19, 50, 36, 44, 27, 14,
+    35, 43, 13, 22, 48, 49, 52, 21, 7, 15, 30, 51, 38, 46, 29, 37,
+    45, 23, 59, 60, 54, 39, 31, 58, 53, 47, 62, 67, 61, 55, 68, 75,
+    56, 70, 63, 76, 69, 57, 83, 78, 91, 84, 77, 71, 92, 86, 65, 94,
+    85, 79, 99, 66, 93, 100, 73, 64, 102, 87, 111, 74, 101, 95, 81, 72,
+    89, 82, 106, 103, 90, 80, 107, 88, 108, 97, 110, 98, 96, 109, 105, 104,
 )
 
 
@@ -139,6 +138,8 @@
     facing = meta_own.at[(z + 4) % 8]
     start(("meta", 8), facing, meta_far.at[0], ring(3))
     start(("meta", 9), facing, meta_far.at[1], ring(-3))
+    start(("meta", 10), meta_own.at[(z + 3) % 8], meta_far.at[2], ring(2))
+    start(("meta", 11), meta_own.at[(z + 5) % 8], meta_far.at[3], ring(-2))
 
     def onehot(slots):
         return slots == lax.broadcasted_iota(jnp.int32, (CAP, TOK), 0).astype(f32)
@@ -151,22 +152,27 @@
             picked = weight * picked
         return picked.astype(bf16)
 
+    def thin(i, p):
+        return (i, p) in ((5, 1), (6, 0), (7, 0), (7, 1), (8, 1))
+
     def take(i, p):
-        if 1 <= i <= 6:
+        if 1 <= i <= 6 and not thin(i, p):
             name, away = ("up", 1) if i % 2 else ("down", -1)
             got = raw.at[i - 1, p]
             arrive((name, p, i), got)
-            if i < 5:
+            if thin(i + 2, p):
+                meta = 2 if i == 3 else 3 if i == 4 else p
+                arrive(("meta", 8 + meta), meta_far.at[meta])
+                far_rows[meta] = choose(raw[i - 1, p], meta_far[meta], p)
+                there = rows.at[p, min(i + 2, 7), mine]
+                start(("thin", p, min(i + 2, 7)), far_rows.at[meta], there, ring(away))
+            elif i < 5:
                 start((name, p, i + 2), got, raw.at[i + 1, p], ring(away))
-            elif p == i - 5:
-                arrive(("meta", 8 + p), meta_far.at[p])
-                far_rows[p] = choose(raw[i - 1, p], meta_far[p], p)
-                start(("last", p), far_rows.at[p], rows.at[p, 7, mine], ring(away))
-        if i == 7:
-            arrive(("last", p), rows.at[p, 7, mine])
+        if p == 0 and 1 <= i <= 6:
+            arrive(("meta", i), meta_in.at[i])
+        if thin(i, p):
+            arrive(("thin", p, i), rows.at[p, i, mine])
         else:
-            if p == 0 and i > 0:
-                arrive(("meta", i), meta_in.at[i])
             block = parts[p][...] if i == 0 else raw[i - 1, p]
             rows[p, i, mine] = choose(block, meta_in[i], p)
         chosen = rows.at[p, i, mine]
@@ -215,42 +221,40 @@
         arrive(("sum+", i), near.at[0, 0, i])
         arrive(("sum-", i), near.at[1, 1, i])
 
-        def total(half):
-            return own[half, x, i] + near[0, half, i].astype(f32) + near[1, half, i].astype(f32)
-
-        qsend[i] = total(1 - yh).astype(bf16)
+        for half in range(2):
+            total = (
+                own[half, x, i] + near[0, half, i].astype(f32) + near[1, half, i].astype(f32)
+            )
+            keep[i, half] = total
+            qsend[i, half] = total.astype(bf16)
         start(("q", i), qsend.at[i], qrecv.at[i], partner)
-        keep[i] = total(yh)
 
     def activate(i):
         arrive(("q", i), qrecv.at[i])
-        total = keep[i] + qrecv[i].astype(f32)
-        a, u, g = total[:, :HID], total[:, HID : 2 * HID], total[:, 2 * HID :]
-        sig = jax.nn.sigmoid(a)
-        silu = a * sig
-        spread[yh, x, i, :, 0:HID] = (silu * u).astype(bf16)
-        spread[yh, x, i, :, HID : 2 * HID] = (g * u * sig * (1.0 + a * (1.0 - sig))).astype(bf16)
-        spread[yh, x, i, :, 2 * HID : 3 * HID] = (g * silu).astype(bf16)
-        made = spread.at[yh, x, i]
-        start(("mate", i), made, made, partner)
-        start(("one+", i), made, made, right)
-        start(("one-", i), made, made, left)
-
-    def share(i):
-        got = spread.at[1 - yh, x, i]
-        arrive(("mate", i), got)
-        start(("two+", i), got, got, right)
-        start(("two-", i), got, got, left)
+        for half in range(2):
+            total = keep[i, half] + qrecv[i, half].astype(f32)
+            a, u, g = total[:, :HID], total[:, HID : 2 * HID], total[:, 2 * HID :]
+            sig = jax.nn.sigmoid(a)
+            silu = a * sig
+            slope = sig * (1.0 + a * (1.0 - sig))
+            spread[half, x, i, :, 0:HID] = (silu * u).astype(bf16)
+            spread[half, x, i, :, HID : 2 * HID] = (g * u * slope).astype(bf16)
+            spread[half, x, i, :, 2 * HID : 3 * HID] = (g * silu).astype(bf16)
+        for half in range(2):
+            made = spread.at[half, x, i]
+            start(("one+", half, i), made, made, right)
+            made = spread.at[1 - half, x, i]
+            start(("one-", 1 - half, i), made, made, left)
 
     def relay(i):
-        arrive(("one+", i), spread.at[yh, xm, i])
-        arrive(("two+", i), spread.at[1 - yh, xm, i])
+        arrive(("one+", 0, i), spread.at[0, xm, i])
         start(("on+", i), spread.at[0, xm, i], spread.at[0, xm, i], right)
-        arrive(("one-", i), spread.at[yh, xp, i])
-        arrive(("two-", i), spread.at[1 - yh, xp, i])
+        arrive(("one-", 1, i), spread.at[1, xp, i])
         start(("on-", i), spread.at[1, xp, i], spread.at[1, xp, i], left)
 
     def row_terms(i):
+        arrive(("one+", 1, i), spread.at[1, xm, i])
+        arrive(("one-", 0, i), spread.at[0, xp, i])
         arrive(("on+", i), spread.at[0, xo, i])
         arrive(("on-", i), spread.at[1, xo, i])
 
@@ -296,7 +300,6 @@
         sum_far,
         sum_near,
         activate,
-        share,
         relay,
         row_terms,
         pair,
@@ -358,17 +361,17 @@
             pltpu.VMEM((3, FEAT, HID), bf16),
             pltpu.VMEM((EXPERTS, 8, TOK), f32),
             pltpu.VMEM((8, 8, TOK), f32),
-            pltpu.VMEM((2, 8, TOK), f32),
+            pltpu.VMEM((4, 8, TOK), f32),
             pltpu.VMEM((6, 2, TOK, FEAT), bf16),
             pltpu.VMEM((2, 8, 4, CAP, FEAT), bf16),
-            pltpu.VMEM((2, CAP, FEAT), bf16),
+            pltpu.VMEM((4, CAP, FEAT), bf16),
             pltpu.VMEM((2, 4, 8, 32, 3 * HID), f32),
             pltpu.VMEM((2, 4, 8, 32, 3 * HID), bf16),
             pltpu.VMEM((2, 8, 32, 3 * HID), bf16),
             pltpu.VMEM((2, 2, 8, 32, 3 * HID), bf16),
-            pltpu.VMEM((8, 32, 3 * HID), f32),
-            pltpu.VMEM((8, 32, 3 * HID), bf16),
-            pltpu.VMEM((8, 32, 3 * HID), bf16),
+            pltpu.VMEM((8, 2, 32, 3 * HID), f32),
+            pltpu.VMEM((8, 2, 32, 3 * HID), bf16),
+            pltpu.VMEM((8, 2, 32, 3 * HID), bf16),
             pltpu.VMEM((2, 4, 8, 32, 3 * HID), bf16),
             pltpu.VMEM((8, 2, CAP, FEAT), bf16),
             pltpu.VMEM((8, 2, CAP, FEAT), f32),

time: 116 us -> 113 us (0.974)
  Pallas kernels: 115 us -> 112 us
    pallas_call x1, Pallas kernels: 112 us -> 110 us  [body(): pl.pallas_call(kernel, out_shape=outs, in_specs=[vmem] * 2 + [anywhere] *...]
where the time goes in v4:
time: 113 us
  Pallas kernels  112 us (99%)
    pallas_call x1, Pallas kernels, body(): pl.pallas_call(kernel, out_shape=outs, in_specs=[vmem] * 2 + [anywhere] *...  110 us
    pallas_call x1, Pallas kernels, body(): pl.pallas_call(hand_on, out_shape=outs, in_specs=[vmem] * 4, out_specs=(v...  2.58 us

profile of v4, /device:TPU:1, one launch (start us, length us, event | category | flops | bytes accessed | tf_op | source)
XLA Modules:
  0.0 112.9 jit_solution(3709276931606816651)
XLA Ops:
  0.6 109.7 %shard_map.102 = (bf16[128,896]{1,0:T(8,128)(2,1)}, bf16[896,256]{1,0:T(8,128)(2,1)}, bf16[896,256]{1,0:T(8,128)(2,1)}, bf16[896,256]{1,0:T(8,128)(2,1)}) custom-call(s32[2,128]{1,0:T(2,128)} %bitcast.2, f32[2,128]{1,0:T(2,128)} %bitcast.3, bf16[128,896]{1,0:T(8,128)(2,1)} %x_in.1, bf16[128,896]{1,0:T(8,128)(2,1)} %c_in.1, bf16[896,256]{1,0:T(8,128)(2,1)} %wg_in.1, ...), custom_call_target="tpu_custom_call" | custom-call | tf_op jit(solution)/shard_map/pallas_call | solution.py:349
  110.3 2.6 %shard_map.103 = (bf16[128,896]{1,0:T(8,128)(2,1)}, bf16[896,256]{1,0:T(8,128)(2,1)}, bf16[896,256]{1,0:T(8,128)(2,1)}, bf16[896,256]{1,0:T(8,128)(2,1)}) custom-call(bf16[128,896]{1,0:T(8,128)(2,1)} %get-tuple-element.8.refs_0_, bf16[896,256]{1,0:T(8,128)(2,1)} %get-tuple-element.9.refs_1_, bf16[896,256]{1,0:T(8,128)(2,1)} %get-tuple-element.10.refs_2_, ...), custom_call_target="tpu_custom_call" | custom-call | tf_op jit(solution)/shard_map/pallas_call | solution.py:393

commit v5 on v4

v5 whole, which is shorter than its diff:
```python
import jax
import jax.numpy as jnp
from jax import lax
from jax.experimental import pallas as pl
from jax.experimental.pallas import tpu as pltpu
from jax.sharding import PartitionSpec as P

EXPERTS = 8
CAP = 64
TOK = 128
FEAT = 896
HID = 256
MESH = pl.DeviceIdType.MESH

SHIFT = (0, -1, 1, -2, 2, -3, 3, 4)
SEMS = 400

UNITS = (
    (0, 0, 64), (1, 0, 64), (2, 0, 64), (3, 0, 32), (3, 32, 32), (4, 0, 32),
    (4, 32, 32), (5, 0, 32), (5, 32, 32), (6, 0, 32), (6, 32, 32), (7, 0, 32),
    (7, 32, 32),
)

ORDER = (
    0, 13, 2, 1, 14, 15, 3, 40, 26, 39, 27, 28, 5, 41, 52, 65,
    16, 18, 54, 67, 30, 53, 66, 31, 7, 78, 43, 57, 29, 32, 80, 44,
    20, 42, 56, 69, 55, 45, 68, 9, 70, 58, 33, 22, 71, 34, 46, 59,
    81, 82, 11, 83, 35, 47, 72, 60, 36, 84, 73, 79, 48, 61, 24, 95,
    49, 74, 62, 75, 97, 37, 38, 94, 86, 85, 63, 50, 87, 96, 88, 51,
    76, 64, 77, 98, 108, 100, 110, 99, 89, 90, 107, 101, 121, 92, 123, 109,
    113, 102, 103, 93, 120, 112, 111, 136, 134, 126, 114, 122, 149, 147, 133, 91,
    125, 124, 115, 146, 116, 139, 127, 105, 135, 162, 152, 137, 160, 138, 128, 129,
    150, 106, 140, 159, 148, 118, 165, 153, 151, 104, 163, 142, 141, 119, 161, 155,
    172, 154, 131, 117, 164, 166, 144, 132, 174, 167, 168, 145, 171, 130, 143, 157,
    170, 180, 158, 176, 169, 178, 156, 182,
)


def dot_nn(left, right):
    return jnp.dot(left, right, preferred_element_type=jnp.float32)


def dot_nt(left, right):
    return lax.dot_general(
        left, right, (((1,), (1,)), ((), ())), preferred_element_type=jnp.float32
    )


def dot_tn(left, right):
    return lax.dot_general(
        left, right, (((0,), (0,)), ((), ())), preferred_element_type=jnp.float32
    )


def kernel(
    ids_ref, gates_ref, x_in, c_in, wg_in, wu_in, wd_in,
    gt_out, gg_out, gu_out, gd_out,
    x_ref, c_ref, wg_ref, wu_ref, wd_ref, gt_ref, wgrads,
    meta_own, meta_in, meta_far, raw, rows, far_rows, own, part, far, near,
    keep, qsend, qrecv, spread, term, kept, term_in, tsend, trecv, final, ret, acc, hots,
    send_sems, recv_sems, load_sems, store_sems,
):
    f32, bf16 = jnp.float32, jnp.bfloat16
    ep = lax.axis_index("ep")
    fs = lax.axis_index("fsdp")
    z, yl, co = ep // 4, (ep // 2) % 2, ep % 2
    yh, x = fs // 4, fs % 4
    xp, xm, xo = (x + 1) % 4, (x + 3) % 4, (x + 2) % 4

    def device(plane, ylo, core):
        return (plane * 4 + ylo * 2 + core, fs)

    def ring(step):
        return device((z + step + 8) % 8, yl, co)

    sibling = device(z, yl, 1 - co)
    across = device(z, 1 - yl, co)
    right, left = (ep, yh * 4 + xp), (ep, yh * 4 + xm)
    partner = (ep, (1 - yh) * 4 + x)
    mine, twin = yl * 2 + co, yl * 2 + (1 - co)
    other, other_twin = (1 - yl) * 2 + co, (1 - yl) * 2 + (1 - co)

    places = {}
    started = []

    def copy(name, source, target, where):
        place = places.setdefault(name, len(places))
        return pltpu.make_async_remote_copy(
            src_ref=source,
            dst_ref=target,
            send_sem=send_sems.at[place],
            recv_sem=recv_sems.at[place],
            device_id=where,
            device_id_type=MESH,
        )

    def start(name, source, target, where):
        made = copy(name, source, target, where)
        made.start()
        started.append(made)

    def arrive(name, target):
        copy(name, target, target, sibling).wait_recv()

    barrier = pltpu.get_barrier_semaphore()
    greeted = [ring(step) for step in range(1, 8)] + [sibling, across, right, left, partner]
    for where in greeted:
        pl.semaphore_signal(barrier, inc=1, device_id=where, device_id_type=MESH)

    loads = [
        pltpu.make_async_copy(source, target, load_sems.at[place])
        for place, (source, target) in enumerate(
            ((x_in, x_ref), (c_in, c_ref), (wg_in, wg_ref), (wu_in, wu_ref), (wd_in, wd_ref))
        )
    ]
    for load in loads:
        load.start()
    parts = (x_ref, c_ref)

    pl.semaphore_wait(barrier, len(greeted))
    for p in range(2):
        loads[p].wait()
        start(("up", p, 1), parts[p], raw.at[0, p], ring(1))
        start(("down", p, 2), parts[p], raw.at[1, p], ring(-1))

    expert = lax.broadcasted_iota(jnp.int32, (EXPERTS, TOK), 0)
    first, second = ids_ref[0:1, :] == expert, ids_ref[1:2, :] == expert
    member = first | second
    ordered = (
        lax.broadcasted_iota(jnp.int32, (TOK, TOK), 0)
        < lax.broadcasted_iota(jnp.int32, (TOK, TOK), 1)
    )
    before = dot_nn(
        jnp.where(member, 1.0, 0.0).astype(bf16), jnp.where(ordered, 1.0, 0.0).astype(bf16)
    )
    slot = jnp.where(member, before, -1.0)
    gate = jnp.where(first, gates_ref[0:1, :], 0.0) + jnp.where(second, gates_ref[1:2, :], 0.0)
    meta_own[...] = jnp.zeros_like(meta_own)
    for e in range(EXPERTS):
        meta_own[e, 0:1, :] = slot[e : e + 1, :]
        meta_own[e, 1:2, :] = gate[e : e + 1, :]
    meta_in[0] = meta_own[z]
    for i in range(1, 7):
        plane = (z - SHIFT[i] + 8) % 8
        start(("meta", i), meta_own.at[plane], meta_in.at[i], device(plane, yl, co))
    facing = meta_own.at[(z + 4) % 8]
    start(("meta", 8), facing, meta_far.at[0], ring(3))
    start(("meta", 9), facing, meta_far.at[1], ring(-3))
    start(("meta", 10), meta_own.at[(z + 3) % 8], meta_far.at[2], ring(2))
    start(("meta", 11), meta_own.at[(z + 5) % 8], meta_far.at[3], ring(-2))

    def onehot(slots):
        return slots == lax.broadcasted_iota(jnp.int32, (CAP, TOK), 0).astype(f32)

    acc[...] = jnp.zeros_like(acc)
    for i in range(8):
        slots = meta_own[(z + SHIFT[i] + 8) % 8, 0:1, :]
        hots[:, i * CAP : (i + 1) * CAP] = jnp.where(onehot(slots), 1.0, 0.0).T.astype(bf16)

    def choose(block, meta, p):
        hot = onehot(meta[0:1, :])
        picked = dot_nn(jnp.where(hot, 1.0, 0.0).astype(bf16), block)
        if p == 1:
            weight = jnp.sum(jnp.where(hot, meta[1:2, :], 0.0), axis=1, keepdims=True)
            picked = weight * picked
        return picked.astype(bf16)

    def thin(i, p):
        return (i, p) in ((5, 1), (6, 0), (7, 0), (7, 1), (8, 1))

    def span(u):
        i, low, count = UNITS[u]
        return i, pl.ds(low, count), pl.ds(low // 2, count // 2)

    def units_of(i):
        return [u for u, unit in enumerate(UNITS) if unit[0] == i]

    def take(u, p):
        i = UNITS[u][0]
        if 1 <= i <= 6 and not thin(i, p):
            name, away = ("up", 1) if i % 2 else ("down", -1)
            got = raw.at[i - 1, p]
            arrive((name, p, i), got)
            if thin(i + 2, p):
                meta = 2 if i == 3 else 3 if i == 4 else p
                arrive(("meta", 8 + meta), meta_far.at[meta])
                far_rows[meta] = choose(raw[i - 1, p], meta_far[meta], p)
                there = rows.at[p, min(i + 2, 7), mine]
                start(("thin", p, min(i + 2, 7)), far_rows.at[meta], there, ring(away))
            elif i < 5:
                start((name, p, i + 2), got, raw.at[i + 1, p], ring(away))
        if p == 0 and 1 <= i <= 6:
            arrive(("meta", i), meta_in.at[i])
        if thin(i, p):
            arrive(("thin", p, i), rows.at[p, i, mine])
        else:
            block = parts[p][...] if i == 0 else raw[i - 1, p]
            rows[p, i, mine] = choose(block, meta_in[i], p)
        for v in units_of(i):
            chosen = rows.at[p, i, mine, span(v)[1]]
            start(("across", p, v), chosen, chosen, across)
            start(("twin", p, v), chosen, chosen, sibling)

    def pass_on(u, p):
        i, slots, _ = span(u)
        got = rows.at[p, i, other, slots]
        arrive(("across", p, u), got)
        start(("forward", p, u), got, got, sibling)

    def complete(u, p):
        i, slots, _ = span(u)
        arrive(("twin", p, u), rows.at[p, i, twin, slots])
        arrive(("forward", p, u), rows.at[p, i, other_twin, slots])

    def block_rows(u, p):
        i, slots, _ = span(u)
        return rows[p, i, :, slots, :].reshape(4 * UNITS[u][2], FEAT)

    def put(u, at, value):
        i, _, q = span(u)
        value = value.reshape(2, 4, UNITS[u][2] // 2, HID)
        own[:, :, i, q, at : at + HID] = value
        part[:, :, i, q, at : at + HID] = value.astype(bf16)

    def multiply_x(u):
        complete(u, 0)
        block = block_rows(u, 0)
        put(u, 0, dot_nn(block, wg_ref[...]))
        put(u, HID, dot_nn(block, wu_ref[...]))

    def multiply_c(u):
        complete(u, 1)
        i, _, q = span(u)
        put(u, 2 * HID, dot_nn(block_rows(u, 1), wd_ref[...]))
        start(("far+", u), part.at[0, xo, i, q], far.at[0, i, q], right)
        start(("far-", u), part.at[1, xo, i, q], far.at[1, i, q], left)
        start(("own+", u), part.at[1, xp, i, q], near.at[0, 1, i, q], right)
        start(("own-", u), part.at[0, xm, i, q], near.at[1, 0, i, q], left)

    def sum_far(u):
        i, _, q = span(u)
        arrive(("far+", u), far.at[0, i, q])
        part[0, xp, i, q] = (own[0, xp, i, q] + far[0, i, q].astype(f32)).astype(bf16)
        start(("sum+", u), part.at[0, xp, i, q], near.at[0, 0, i, q], right)
        arrive(("far-", u), far.at[1, i, q])
        part[1, xm, i, q] = (own[1, xm, i, q] + far[1, i, q].astype(f32)).astype(bf16)
        start(("sum-", u), part.at[1, xm, i, q], near.at[1, 1, i, q], left)

    def sum_near(u):
        i, _, q = span(u)
        arrive(("own+", u), near.at[0, 1, i, q])
        arrive(("own-", u), near.at[1, 0, i, q])
        arrive(("sum+", u), near.at[0, 0, i, q])
        arrive(("sum-", u), near.at[1, 1, i, q])
        for half in range(2):
            total = (
                own[half, x, i, q]
                + near[0, half, i, q].astype(f32)
                + near[1, half, i, q].astype(f32)
            )
            keep[i, half, q] = total
            qsend[i, half, q] = total.astype(bf16)
        start(("q", u), qsend.at[i, :, q], qrecv.at[i, :, q], partner)

    def activate(u):
        i, _, q = span(u)
        arrive(("q", u), qrecv.at[i, :, q])
        for half in range(2):
            total = keep[i, half, q] + qrecv[i, half, q].astype(f32)
            a, up, g = total[:, :HID], total[:, HID : 2 * HID], total[:, 2 * HID :]
            sig = jax.nn.sigmoid(a)
            silu = a * sig
            slope = sig * (1.0 + a * (1.0 - sig))
            spread[half, x, i, q, 0:HID] = (silu * up).astype(bf16)
            spread[half, x, i, q, HID : 2 * HID] = (g * up * slope).astype(bf16)
            spread[half, x, i, q, 2 * HID : 3 * HID] = (g * silu).astype(bf16)
        for half in range(2):
            made = spread.at[half, x, i, q]
            start(("one+", half, u), made, made, right)
            made = spread.at[1 - half, x, i, q]
            start(("one-", 1 - half, u), made, made, left)

    def relay(u):
        i, _, q = span(u)
        got = spread.at[0, xm, i, q]
        arrive(("one+", 0, u), got)
        start(("on+", u), got, got, right)
        got = spread.at[1, xp, i, q]
        arrive(("one-", 1, u), got)
        start(("on-", u), got, got, left)

    def row_terms(u):
        i, slots, q = span(u)
        arrive(("one+", 1, u), spread.at[1, xm, i, q])
        arrive(("one-", 0, u), spread.at[0, xp, i, q])
        arrive(("on+", u), spread.at[0, xo, i, q])
        arrive(("on-", u), spread.at[1, xo, i, q])
        count = UNITS[u][2]

        def product(core):
            held = spread[:, pl.ds(2 * core, 2), i, q].reshape(2 * count, 3 * HID)
            value = dot_nt(held[:, HID : 2 * HID], wg_ref[...])
            value = value + dot_nt(held[:, 2 * HID :], wu_ref[...])
            return value.reshape(2, count, FEAT)

        term[i, :, slots] = product(1 - co).astype(bf16)
        start(("core", u), term.at[i, :, slots], term_in.at[i, :, slots], sibling)
        kept[i, :, slots] = product(co)

    def pair(u):
        i, slots, _ = span(u)
        arrive(("core", u), term_in.at[i, :, slots])
        tsend[i, slots] = (
            kept[i, 1 - yl, slots] + term_in[i, 1 - yl, slots].astype(f32)
        ).astype(bf16)
        start(("ypair", u), tsend.at[i, slots], trecv.at[i, slots], across)

    def back(u):
        i, slots, _ = span(u)
        arrive(("ypair", u), trecv.at[i, slots])
        value = kept[i, yl, slots] + term_in[i, yl, slots].astype(f32)
        value = (value + trecv[i, slots].astype(f32)).astype(bf16)
        if i == 0:
            ret[0, slots] = value
            return
        final[i, slots] = value
        home = SHIFT.index(-SHIFT[i]) if i < 7 else 7
        name = ("ret", home, UNITS[u][1])
        start(name, final.at[i, slots], ret.at[home, slots], ring(SHIFT[i]))

    def weight_grads(u):
        i = UNITS[u][0]

        def joined(pieces):
            return pieces[0] if len(pieces) == 1 else jnp.concatenate(pieces, axis=0)

        own_units = units_of(i)
        held = joined(
            [spread[:, :, i, span(v)[2]].reshape(4 * UNITS[v][2], 3 * HID) for v in own_units]
        )
        block = joined([block_rows(v, 0) for v in own_units])
        acc[0] += dot_tn(held[:, HID : 2 * HID], block)
        acc[1] += dot_tn(held[:, 2 * HID :], block)
        acc[2] += dot_tn(held[:, :HID], joined([block_rows(v, 1) for v in own_units]))

    stores = []

    def finish(_):
        for place, target in enumerate((gg_out, gu_out, gd_out)):
            wgrads[place] = acc[place].T.astype(bf16)
            stores.append(pltpu.make_async_copy(wgrads.at[place], target, store_sems.at[place]))
            stores[-1].start()

    run = (
        lambda u: take(u, 0),
        lambda u: take(u, 1),
        lambda u: pass_on(u, 0),
        lambda u: pass_on(u, 1),
        multiply_x,
        multiply_c,
        sum_far,
        sum_near,
        activate,
        relay,
        row_terms,
        pair,
        back,
        weight_grads,
        finish,
    )
    loaded = False
    for item in ORDER:
        step, u = item // len(UNITS), item % len(UNITS)
        if run[step] is multiply_x and not loaded:
            for load in loads[2:]:
                load.wait()
            loaded = True
        run[step](u)

    for made in started:
        made.wait_send()
    for i, low, count in UNITS:
        if i > 0:
            arrive(("ret", i, low), ret.at[i, pl.ds(low, count)])
    gt_ref[...] = dot_nn(hots[...], ret[...].reshape(8 * CAP, FEAT)).astype(bf16)
    stores.append(pltpu.make_async_copy(gt_ref, gt_out, store_sems.at[3]))
    stores[-1].start()
    for store in stores:
        store.wait()


def hand_on(*refs):
    sems = refs[8]
    copies = [pltpu.make_async_copy(refs[k], refs[4 + k], sems.at[k]) for k in range(4)]
    for item in copies:
        item.start()
    for item in copies:
        item.wait()


def body(tokens, cotangent, route_gates, expert_ids, w_gate, w_up, w_down):
    bf16, f32 = jnp.bfloat16, jnp.float32
    vmem = pl.BlockSpec(memory_space=pltpu.VMEM)
    anywhere = pl.BlockSpec(memory_space=pl.ANY)
    shape = jax.ShapeDtypeStruct
    outs = (shape((TOK, FEAT), bf16),) + (shape((FEAT, HID), bf16),) * 3
    results = pl.pallas_call(
        kernel,
        out_shape=outs,
        in_specs=[vmem] * 2 + [anywhere] * 5,
        out_specs=(anywhere,) * 4,
        scratch_shapes=[
            pltpu.VMEM((TOK, FEAT), bf16),
            pltpu.VMEM((TOK, FEAT), bf16),
            pltpu.VMEM((FEAT, HID), bf16),
            pltpu.VMEM((FEAT, HID), bf16),
            pltpu.VMEM((FEAT, HID), bf16),
            pltpu.VMEM((TOK, FEAT), bf16),
            pltpu.VMEM((3, FEAT, HID), bf16),
            pltpu.VMEM((EXPERTS, 8, TOK), f32),
            pltpu.VMEM((8, 8, TOK), f32),
            pltpu.VMEM((4, 8, TOK), f32),
            pltpu.VMEM((6, 2, TOK, FEAT), bf16),
            pltpu.VMEM((2, 8, 4, CAP, FEAT), bf16),
            pltpu.VMEM((4, CAP, FEAT), bf16),
            pltpu.VMEM((2, 4, 8, 32, 3 * HID), f32),
            pltpu.VMEM((2, 4, 8, 32, 3 * HID), bf16),
            pltpu.VMEM((2, 8, 32, 3 * HID), bf16),
            pltpu.VMEM((2, 2, 8, 32, 3 * HID), bf16),
            pltpu.VMEM((8, 2, 32, 3 * HID), f32),
            pltpu.VMEM((8, 2, 32, 3 * HID), bf16),
            pltpu.VMEM((8, 2, 32, 3 * HID), bf16),
            pltpu.VMEM((2, 4, 8, 32, 3 * HID), bf16),
            pltpu.VMEM((8, 2, CAP, FEAT), bf16),
            pltpu.VMEM((8, 2, CAP, FEAT), f32),
            pltpu.VMEM((8, 2, CAP, FEAT), bf16),
            pltpu.VMEM((8, CAP, FEAT), bf16),
            pltpu.VMEM((8, CAP, FEAT), bf16),
            pltpu.VMEM((8, CAP, FEAT), bf16),
            pltpu.VMEM((8, CAP, FEAT), bf16),
            pltpu.VMEM((3, HID, FEAT), f32),
            pltpu.VMEM((TOK, 8 * CAP), bf16),
            pltpu.SemaphoreType.DMA((SEMS,)),
            pltpu.SemaphoreType.DMA((SEMS,)),
            pltpu.SemaphoreType.DMA((5,)),
            pltpu.SemaphoreType.DMA((4,)),
        ],
        compiler_params=pltpu.CompilerParams(
            collective_id=0, has_side_effects=True, vmem_limit_bytes=60 * 1024 * 1024
        ),
    )(expert_ids.T, route_gates.T, tokens, cotangent, w_gate, w_up, w_down)
    return pl.pallas_call(
        hand_on,
        out_shape=outs,
        in_specs=[anywhere] * 4,
        out_specs=(vmem,) * 4,
        scratch_shapes=[pltpu.SemaphoreType.DMA((4,))],
    )(*results)


def solution(mesh):
    placed = (
        P("ep", "fsdp"),
        P("ep", "fsdp"),
        P("ep", None),
        P("ep", None),
        P("fsdp", "ep"),
        P("fsdp", "ep"),
        P("fsdp", "ep"),
    )
    return jax.shard_map(
        body,
        mesh=mesh,
        in_specs=placed,
        out_specs=(P("ep", "fsdp"), P("fsdp", "ep"), P("fsdp", "ep"), P("fsdp", "ep")),
        check_vma=False,
    )
```

time: 113 us -> 114 us (level)
  no operation moved by 1% of the time
where the time goes in v5:
time: 114 us
  Pallas kernels  113 us (99%)
    pallas_call x1, Pallas kernels, body(): pl.pallas_call(kernel, out_shape=outs, in_specs=[vmem] * 2 + [anywhere] *...  110 us
    pallas_call x1, Pallas kernels, body(): pl.pallas_call(hand_on, out_shape=outs, in_specs=[anywhere] * 4, out_spec...  2.6 us

profile of v5, /device:TPU:1, one launch (start us, length us, event | category | flops | bytes accessed | tf_op | source)
XLA Modules:
  0.0 113.5 jit_solution(3817666751892298988)
XLA Ops:
  0.6 110.1 %shard_map.102 = (bf16[128,896]{1,0:T(8,128)(2,1)}, bf16[896,256]{1,0:T(8,128)(2,1)}, bf16[896,256]{1,0:T(8,128)(2,1)}, bf16[896,256]{1,0:T(8,128)(2,1)}) custom-call(s32[2,128]{1,0:T(2,128)} %bitcast.2, f32[2,128]{1,0:T(2,128)} %bitcast.3, bf16[128,896]{1,0:T(8,128)(2,1)} %x_in.1, bf16[128,896]{1,0:T(8,128)(2,1)} %c_in.1, bf16[896,256]{1,0:T(8,128)(2,1)} %wg_in.1, ...), custom_call_target="tpu_custom_call" | custom-call | tf_op jit(solution)/shard_map/pallas_call | solution.py:407
  110.8 2.6 %shard_map.103 = (bf16[128,896]{1,0:T(8,128)(2,1)}, bf16[896,256]{1,0:T(8,128)(2,1)}, bf16[896,256]{1,0:T(8,128)(2,1)}, bf16[896,256]{1,0:T(8,128)(2,1)}) custom-call(bf16[128,896]{1,0:T(8,128)(2,1)} %get-tuple-element.8.refs_0_, bf16[896,256]{1,0:T(8,128)(2,1)} %get-tuple-element.9.refs_1_, bf16[896,256]{1,0:T(8,128)(2,1)} %get-tuple-element.10.refs_2_, ...), custom_call_target="tpu_custom_call" | custom-call | tf_op jit(solution)/shard_map/pallas_call | solution.py:452

commit v6 on v4

--- a/solution.py
+++ b/solution.py
@@ -45,8 +45,8 @@
 
 def kernel(
     ids_ref, gates_ref, x_in, c_in, wg_in, wu_in, wd_in,
-    gt_out, gg_out, gu_out, gd_out,
-    x_ref, c_ref, wg_ref, wu_ref, wd_ref, gt_ref, wgrads,
+    ret_out, hot_out, gg_out, gu_out, gd_out,
+    x_ref, c_ref, wg_ref, wu_ref, wd_ref, hot_ref, wgrads,
     meta_own, meta_in, meta_far, raw, rows, far_rows, own, part, far, near,
     keep, qsend, qrecv, spread, term, kept, term_in, tsend, trecv, final, ret, acc,
     send_sems, recv_sems, load_sems, store_sems,
@@ -323,20 +323,23 @@
     for i in range(8):
         slots = meta_own[(z + SHIFT[i] + 8) % 8, 0:1, :]
         hots.append(jnp.where(onehot(slots), 1.0, 0.0).astype(bf16))
-    hots = jnp.concatenate(hots, axis=0)
+    hot_ref[...] = jnp.concatenate(hots, axis=0)
+    stores.append(pltpu.make_async_copy(hot_ref, hot_out, store_sems.at[3]))
+    stores[-1].start()
     for made in started:
         made.wait_send()
-    for i in range(1, 8):
-        arrive(("ret", i), ret.at[i])
-    gt_ref[...] = dot_tn(hots, ret[...].reshape(8 * CAP, FEAT)).astype(bf16)
-    stores.append(pltpu.make_async_copy(gt_ref, gt_out, store_sems.at[3]))
-    stores[-1].start()
+    for i in range(8):
+        if i > 0:
+            arrive(("ret", i), ret.at[i])
+        stores.append(pltpu.make_async_copy(ret.at[i], ret_out.at[i], store_sems.at[4 + i]))
+        stores[-1].start()
     for store in stores:
         store.wait()
 
 
-def hand_on(*refs):
-    for source, target in zip(refs[:4], refs[4:]):
+def combine(ret, hot, gg, gu, gd, gt_out, gg_out, gu_out, gd_out):
+    gt_out[...] = dot_tn(hot[...], ret[...].reshape(8 * CAP, FEAT)).astype(jnp.bfloat16)
+    for source, target in ((gg, gg_out), (gu, gu_out), (gd, gd_out)):
         target[...] = source[...]
 
 
@@ -346,18 +349,19 @@
     anywhere = pl.BlockSpec(memory_space=pl.ANY)
     shape = jax.ShapeDtypeStruct
     outs = (shape((TOK, FEAT), bf16),) + (shape((FEAT, HID), bf16),) * 3
+    sent = (shape((8, CAP, FEAT), bf16), shape((8 * CAP, TOK), bf16)) + outs[1:]
     results = pl.pallas_call(
         kernel,
-        out_shape=outs,
+        out_shape=sent,
         in_specs=[vmem] * 2 + [anywhere] * 5,
-        out_specs=(anywhere,) * 4,
+        out_specs=(anywhere,) * 5,
         scratch_shapes=[
             pltpu.VMEM((TOK, FEAT), bf16),
             pltpu.VMEM((TOK, FEAT), bf16),
             pltpu.VMEM((FEAT, HID), bf16),
             pltpu.VMEM((FEAT, HID), bf16),
             pltpu.VMEM((FEAT, HID), bf16),
-            pltpu.VMEM((TOK, FEAT), bf16),
+            pltpu.VMEM((8 * CAP, TOK), bf16),
             pltpu.VMEM((3, FEAT, HID), bf16),
             pltpu.VMEM((EXPERTS, 8, TOK), f32),
             pltpu.VMEM((8, 8, TOK), f32),
@@ -384,16 +388,16 @@
             pltpu.SemaphoreType.DMA((SEMS,)),
             pltpu.SemaphoreType.DMA((SEMS,)),
             pltpu.SemaphoreType.DMA((5,)),
-            pltpu.SemaphoreType.DMA((4,)),
+            pltpu.SemaphoreType.DMA((12,)),
         ],
         compiler_params=pltpu.CompilerParams(
             collective_id=0, has_side_effects=True, vmem_limit_bytes=60 * 1024 * 1024
         ),
     )(expert_ids.T, route_gates.T, tokens, cotangent, w_gate, w_up, w_down)
     return pl.pallas_call(
-        hand_on,
+        combine,
         out_shape=outs,
-        in_specs=[vmem] * 4,
+        in_specs=[vmem] * 5,
         out_specs=(vmem,) * 4,
     )(*results)
 

time: 113 us -> 113 us (level)
  no operation moved by 1% of the time
where the time goes in v6:
time: 113 us
  Pallas kernels  112 us (99%)
    pallas_call x1, Pallas kernels, body(): pl.pallas_call(kernel, out_shape=sent, in_specs=[vmem] * 2 + [anywhere] *...  109 us
    pallas_call x1, Pallas kernels, body(): pl.pallas_call(combine, out_shape=outs, in_specs=[vmem] * 5, out_specs=(v...  3.07 us

profile of v6, /device:TPU:1, one launch (start us, length us, event | category | flops | bytes accessed | tf_op | source)
XLA Modules:
  0.0 113.1 jit_solution(8883053690234889606)
XLA Ops:
  0.6 109.4 %shard_map.102 = (bf16[8,64,896]{2,1,0:T(8,128)(2,1)}, bf16[512,128]{1,0:T(8,128)(2,1)}, bf16[896,256]{1,0:T(8,128)(2,1)}, bf16[896,256]{1,0:T(8,128)(2,1)}, bf16[896,256]{1,0:T(8,128)(2,1)}) custom-call(s32[2,128]{1,0:T(2,128)} %bitcast.2, f32[2,128]{1,0:T(2,128)} %bitcast.3, bf16[128,896]{1,0:T(8,128)(2,1)} %x_in.1, bf16[128,896]{1,0:T(8,128)(2,1)} %c_in.1, ...), custom_call_target="tpu_custom_call" | custom-call | tf_op jit(solution)/shard_map/pallas_call | solution.py:353
  110.0 3.1 %shard_map.103 = (bf16[128,896]{1,0:T(8,128)(2,1)}, bf16[896,256]{1,0:T(8,128)(2,1)}, bf16[896,256]{1,0:T(8,128)(2,1)}, bf16[896,256]{1,0:T(8,128)(2,1)}) custom-call(bf16[8,64,896]{2,1,0:T(8,128)(2,1)} %get-tuple-element.9.ret, bf16[512,128]{1,0:T(8,128)(2,1)} %get-tuple-element.10.hot, bf16[896,256]{1,0:T(8,128)(2,1)} %get-tuple-element.11.gg, ...), custom_call_target="tpu_custom_call" | custom-call | tf_op jit(solution)/shard_map/pallas_call | solution.py:397
